TPU v7x, 128 devices: a whole 4x4x4 slice. The times are simulated.
128 devices in a mesh: row: 16 (over z, y_hi, core), col: 8 (over y_lo, x).
Axes of the slice: x: 4, y: 4 (y_hi: 2, y_lo: 2; y = y_hi * 2 + y_lo), z: 4, core: 2. Of those that a mesh axis runs over, the one named last changes fastest.
Arguments:
- tokens: bfloat16 [16384, 2048], P('row', 'col')
- segment_ids: int32 [16384], replicated, may hold values from 0 to 23, as said below
- norm_one: bfloat16 [2048], replicated, may hold values from 0.5 to 1.5
- w_query: bfloat16 [2048, 2048], P('row', 'col'), may hold values from -0.125 to 0.125
- w_key: bfloat16 [2048, 256], replicated, may hold values from -0.125 to 0.125
- w_value: bfloat16 [2048, 256], replicated, may hold values from -0.125 to 0.125
- w_out: bfloat16 [2048, 2048], P('col', 'row'), may hold values from -0.75 to 0.75
- norm_two: bfloat16 [2048], replicated, may hold values from 0.5 to 1.5
- w_gate: bfloat16 [2048, 5632], P('row', 'col'), may hold values from -0.125 to 0.125
- w_up: bfloat16 [2048, 5632], P('row', 'col'), may hold values from -0.125 to 0.125
- w_down: bfloat16 [5632, 2048], P('col', 'row'), may hold values from -0.15625 to 0.15625
- cotangent: bfloat16 [16384, 2048], P('row', 'col'), may hold values from -6 to 6
Outputs:
- mixed: bfloat16 [16384, 2048], P('row', 'col')
- input_grad: float32 [16384, 2048], P('row', 'col')
- query_grad: float32 [2048, 2048], P('row', 'col')
- key_grad: float32 [2048, 256], replicated
- value_grad: float32 [2048, 256], replicated
- out_grad: float32 [2048, 2048], P('col', 'row')
- gate_grad: float32 [2048, 5632], P('row', 'col')
- up_grad: float32 [2048, 5632], P('row', 'col')
- down_grad: float32 [5632, 2048], P('col', 'row')
- norm_one_grad: float32 [2048], replicated
- norm_two_grad: float32 [2048], replicated
- stream_rms: float32 [3], replicated
Inputs may be any that keep to these rules, and one draw needn't show every extreme that they name: `segment_ids`: Non-decreasing, rising by at most one from a token to the next; every sequence of 2048 tokens holds exactly three documents, numbered 3 s, 3 s + 1 and 3 s + 2 for sequence s; the middle one covers its positions 768 to 1279.
All inputs are finite; a program needn't handle non-finite values.
Results may differ from a plain program's by a relative error of at most 0.02.
Values may be sent and summed in bfloat16 or wider, within the bound.
A program may use at most 256 MiB of HBM per device.

v0:
```python
import functools
import math

import jax
import jax.numpy as jnp
from jax import lax
from jax.experimental import pallas as pl
from jax.experimental.pallas import tpu as pltpu
from jax.sharding import PartitionSpec as P

BF16 = jnp.bfloat16
F32 = jnp.float32
HEAD = 64
eps = 1e-05
MESH = pl.DeviceIdType.MESH
ANY = pl.BlockSpec(memory_space=pl.ANY)
CHUNK = 256
T = 512


class Place:
    def __init__(self):
        row = lax.axis_index("row")
        col = lax.axis_index("col")
        self.z = row // 4
        self.yh = (row // 2) % 2
        self.core = row % 2
        self.yl = col // 4
        self.x = col % 4
        self.y = self.yh * 2 + self.yl
        self.quarter = self.core * 2 + self.yl

    def at(self, z, y, core, x):
        return {"row": z * 4 + (y // 2) * 2 + core, "col": (y % 2) * 4 + x}

    def by_x(self, d):
        return self.at(self.z, self.y, self.core, (self.x + d) % 4)

    def by_z(self, d):
        return self.at((self.z + d) % 4, self.y, self.core, self.x)

    def by_y(self, d):
        return self.at(self.z, (self.y + d) % 4, self.core, self.x)

    def partner(self):
        return self.at(self.z, self.y, 1 - self.core, self.x)

    def by_quarter(self, d):
        q = (self.quarter + d) % 4
        return self.at(self.z, self.yh * 2 + q % 2, q // 2, self.x)


def greet(peers):
    barrier = pltpu.get_barrier_semaphore()
    for peer in peers:
        pl.semaphore_signal(barrier, inc=1, device_id=peer, device_id_type=MESH)
    pl.semaphore_wait(barrier, len(peers))


def send(src, dst, sems, k, peer):
    return pltpu.make_async_remote_copy(
        src_ref=src, dst_ref=dst, send_sem=sems[0].at[k], recv_sem=sems[1].at[k],
        device_id=peer, device_id_type=MESH,
    )


def each(count, act):
    def step(i, carry):
        act(i)
        return carry

    lax.fori_loop(0, count, step, 0)


def perm_row(z, y, core):
    yh = y // 2
    return ((z % 2) * 2 + yh) * 512 + (z // 2) * 256 + core * 128


def reshard_in(me, src, full, sems, base, lsem):
    def chunk(q):
        return src.at[pl.ds(pl.multiple_of(jnp.where(me.core == 0, q, 3 - q) * CHUNK, CHUNK), CHUNK)]

    half = pl.multiple_of(me.core * CHUNK, CHUNK)
    place = full.at[pl.ds(half, CHUNK), pl.ds(pl.multiple_of(me.x * 512 + me.yl * 256, 256), 256)]
    copies = []
    for d in (1, 2, 3):
        copies.append(send(chunk((me.quarter + d) % 4), place, sems, base + d, me.by_quarter(d)))
    local = pltpu.make_async_copy(chunk(me.quarter), place, lsem)
    return copies, local


def ring_gather(me, full, sems):
    x = me.x
    right, left = me.by_x(1), me.by_x(3)
    xl, xr = (x + 3) % 4, (x + 1) % 4
    h = full.shape[1] // 2
    one = [
        send(full.at[x], full.at[x], sems, 0, right),
        send(full.at[x], full.at[x], sems, 1, left),
    ]
    two = [
        send(full.at[xl, pl.ds(0, h)], full.at[xl, pl.ds(0, h)], sems, 2, right),
        send(full.at[xr, pl.ds(h, h)], full.at[xr, pl.ds(h, h)], sems, 3, left),
    ]
    return one, two


class Spread:
    def __init__(self, me, src, slot, z_first, sems, lsem):
        self.me, self.src, self.slot, self.z_first, self.sems, self.lsem = me, src, slot, z_first, sems, lsem

    def local(self):
        me = self.me
        return pltpu.make_async_copy(self.src, self.slot(me.z, me.y, me.core), self.lsem)

    def first(self, i):
        me = self.me
        peer = me.by_z(i + 1) if self.z_first else me.by_y(i + 1)
        return send(self.src, self.slot(me.z, me.y, me.core), self.sems, i, peer)

    def line(self, k):
        me = self.me
        if self.z_first:
            return self.slot((me.z + 4 - k) % 4, me.y, me.core)
        return self.slot(me.z, (me.y + 4 - k) % 4, me.core)

    def second(self, k, i):
        me = self.me
        peer = me.by_y(i + 1) if self.z_first else me.by_z(i + 1)
        block = self.line(k)
        return send(block, block, self.sems, 3 + k * 3 + i, peer)

    def third(self, i):
        me = self.me
        if self.z_first:
            block = self.slot((me.z + 4 - i // 4) % 4, (me.y + 4 - i % 4) % 4, me.core)
        else:
            block = self.slot((me.z + 4 - i % 4) % 4, (me.y + 4 - i // 4) % 4, me.core)
        return send(block, block, self.sems, 15 + i, me.partner())

    def start(self):
        self.local().start()
        each(3, lambda i: self.first(i).start())

    def turn(self):
        self.local().wait()
        each(3, lambda i: self.second(0, i).start())
        self.third(0).start()

        def arrived(k):
            self.first(k).wait_recv()
            each(3, lambda i: self.second(k + 1, i).start())
            self.third((k + 1) * 4).start()

        each(3, arrived)

    def cross(self):
        def arrived(j):
            k, i = j // 3, j % 3
            self.second(k, i).wait_recv()
            self.third(k * 4 + i + 1).start()

        each(12, arrived)

    def finish(self):
        each(16, lambda i: self.third(i).wait_recv())
        each(3, lambda i: self.first(i).wait_send())
        each(12, lambda j: self.second(j // 3, j % 3).wait_send())
        each(16, lambda i: self.third(i).wait_send())


def weight_slots(q, o, g, u, d):
    def ds(start, size):
        return pl.ds(pl.multiple_of(start, 128), size)

    return (
        lambda z, y, c: q.at[ds(perm_row(z, y, c), 128), ds((y % 2) * 256, 256)],
        lambda z, y, c: o.at[ds((y % 2) * 256, 256), ds(perm_row(z, y, c), 128)],
        lambda z, y, c: g.at[y % 2, ds(perm_row(z, y, c), 128)],
        lambda z, y, c: u.at[y % 2, ds(perm_row(z, y, c), 128)],
        lambda z, y, c: d.at[y % 2, :, ds(perm_row(z, y, c), 128)],
    )


def greet_all(me):
    peers = [me.by_x(i) for i in (1, 2, 3)]
    peers += [me.by_z(i) for i in (1, 2, 3)] + [me.by_y(i) for i in (1, 2, 3)]
    peers += [me.by_quarter(i) for i in (1, 2, 3)]
    greet(peers)


def dot_plain(left, right):
    return jnp.dot(left, right, preferred_element_type=F32)


def dot_tn(left, right):
    return lax.dot_general(left, right, (((0,), (0,)), ((), ())), preferred_element_type=F32)


def dot_nt(left, right):
    return lax.dot_general(left, right, (((1,), (1,)), ((), ())), preferred_element_type=F32)


def lanes(start, size):
    return pl.ds(pl.multiple_of(start, 128), size)


class Ring:
    def __init__(self, me, full, rows, sems, base):
        x = me.x
        right, left = me.by_x(1), me.by_x(3)
        xl, xr = (x + 3) % 4, (x + 1) % 4

        def at(b, off, size):
            return full.at[rows, lanes(b * 512 + off, size)]

        self.one = [
            send(at(x, 0, 512), at(x, 0, 512), sems, base + 0, right),
            send(at(x, 0, 512), at(x, 0, 512), sems, base + 1, left),
        ]
        self.two = [
            send(at(xl, 0, 256), at(xl, 0, 256), sems, base + 2, right),
            send(at(xr, 256, 256), at(xr, 256, 256), sems, base + 3, left),
        ]

    def start(self):
        for c in self.one:
            c.start()

    def turn(self):
        for a, b in zip(self.one, self.two):
            a.wait_recv()
            b.start()

    def finish(self):
        for a in self.one:
            a.wait_send()
        for b in self.two:
            b.wait()


class RingSum:
    def __init__(self, me, part, rows, hop, got, sems, base):
        x = me.x
        self.part, self.rows, self.hop, self.got, self.x = part, rows, hop, got, x
        right, left = me.by_x(1), me.by_x(3)
        far, xr, xl = (x + 2) % 4, (x + 1) % 4, (x + 3) % 4
        self.xr, self.xl = xr, xl

        def at(b, off):
            return part.at[rows, lanes(b * 512 + off, 256)]

        self.one = [
            send(at(far, 0), hop.at[0], sems, base + 0, right),
            send(at(far, 256), hop.at[1], sems, base + 1, left),
            send(at(xr, 256), got.at[0, :, pl.ds(256, 256)], sems, base + 2, right),
            send(at(xl, 0), got.at[1, :, pl.ds(0, 256)], sems, base + 3, left),
        ]
        self.two = [
            send(at(xr, 0), got.at[0, :, pl.ds(0, 256)], sems, base + 4, right),
            send(at(xl, 256), got.at[1, :, pl.ds(256, 256)], sems, base + 5, left),
        ]

    def start(self):
        for c in self.one:
            c.start()

    def turn(self):
        for k, (b, off) in enumerate(((self.xr, 0), (self.xl, 256))):
            self.one[k].wait_recv()
            cols = lanes(b * 512 + off, 256)
            total = self.part[self.rows, cols].astype(F32) + self.hop[k].astype(F32)
            self.part[self.rows, cols] = total.astype(BF16)
            self.two[k].start()

    def finish(self):
        for k in (2, 3):
            self.one[k].wait_recv()
        for c in self.two:
            c.wait_recv()
        own = self.part[self.rows, lanes(self.x * 512, 512)].astype(F32)
        return own + self.got[0].astype(F32) + self.got[1].astype(F32)

    def drain(self):
        for c in self.one + self.two:
            c.wait_send()


def rope_rows(a, b, cosine, sine):
    return a * cosine - b * sine, b * cosine + a * sine


def document_starts(ids, seq, place):
    ids = ids[seq]

    def below(number):
        hit = (ids < number).astype(F32)
        return jnp.sum(jnp.sum(hit, 1, keepdims=True), 0, keepdims=True)

    second, third = below(3 * seq + 1).astype(jnp.int32), below(3 * seq + 2).astype(jnp.int32)
    return jnp.where(place >= third, third, jnp.where(place >= second, second, 0))


ORIGINAL = [(p % 2) * 4 + p // 2 for p in range(8)]


def device_order_row(ref):
    return jnp.concatenate([ref[:, b * 256:(b + 1) * 256].astype(F32) for b in ORIGINAL], 1)


def rms_rows(src, gain, dst, rstd):
    def step(k, carry):
        rows = pl.ds(pl.multiple_of(k * 64, 64), 64)
        v = src[rows, :].astype(F32)
        r = lax.rsqrt(jnp.sum(v * v, 1, keepdims=True) * (1.0 / 2048.0) + eps)
        rstd[rows, :] = r
        dst[rows, :] = (v * r * gain).astype(BF16)
        return carry

    lax.fori_loop(0, src.shape[0] // 64, step, 0)


def forward_kernel(
    tok, cot, wq_s, wo_s, wg_s, wu_s, wd_s, w_key, w_value, gain1, ids,
    xf, cf, mf, wq, wo, wg, wu, wd, qt, kvt, lse, ot, x1, h1, r1,
    part, hop, got, acc, mx, sm, kr, o_r, kv_tmp,
    a_s, a_r, w_s, w_r, lsem,
):
    me = Place()
    x = me.x
    acts = (a_s, a_r)
    greet_all(me)
    slots = weight_slots(wq, wo, wg, wu, wd)
    first_z = (True, True, True, False, False)
    spreads = [
        Spread(me, src, slots[n], first_z[n], (w_s.at[n], w_r.at[n]), lsem.at[2 + n])
        for n, src in enumerate((wq_s, wo_s, wg_s, wu_s, wd_s))
    ]
    in_copies, in_local = reshard_in(me, tok, xf, acts, 0, lsem.at[0])
    cot_copies, cot_local = reshard_in(me, cot, cf, acts, 4, lsem.at[1])
    for c in in_copies + [in_local]:
        c.start()
    for s in spreads:
        s.start()
    for c in cot_copies + [cot_local]:
        c.start()
    seq = me.z * 2 + me.yh
    chunk_of = (me.quarter, 7 - me.quarter)
    lane = lax.broadcasted_iota(jnp.int32, (1, CHUNK), 1)
    places = [c * CHUNK + lane for c in chunk_of]
    starts = [document_starts(ids, seq, p) for p in places]
    pos = jnp.concatenate([p - s for p, s in zip(places, starts)], 1).astype(F32)
    turn = lax.broadcasted_iota(jnp.int32, (32, 1), 0).astype(F32)
    angle = jnp.exp(-math.log(10000.0) * turn / 32.0) * pos
    cosine, sine = jnp.cos(angle), jnp.sin(angle)
    gain = device_order_row(gain1)

    for c in in_copies:
        c.wait_recv()
    in_local.wait()
    ring_tok = Ring(me, xf, pl.ds(0, T), acts, 8)
    ring_tok.start()
    spreads[0].turn()
    spreads[1].turn()
    for c in cot_copies:
        c.wait_recv()
    cot_local.wait()
    ring_tok.turn()
    ring_cot = Ring(me, cf, pl.ds(0, T), acts, 12)
    ring_cot.start()
    spreads[0].cross()
    for s in spreads[2:]:
        s.turn()
    ring_tok.finish()
    for c in in_copies + cot_copies:
        c.wait_send()

    rms_rows(xf, gain, h1, r1)
    spreads[0].finish()
    for n, w in enumerate((w_key, w_value)):
        total = None
        for p, b in enumerate(ORIGINAL):
            d = dot_plain(h1[:, p * 256:(p + 1) * 256], w[b * 256:(b + 1) * 256, :])
            total = d if total is None else total + d
        kv_tmp[n * 256:(n + 1) * 256, :] = total.T
    for g in (0, 1):
        head = pl.multiple_of((2 * g + x // 2) * HEAD, HEAD)
        a, b = rope_rows(kv_tmp[pl.ds(head, 32), :], kv_tmp[pl.ds(head + 32, 32), :], cosine, sine)
        v = kv_tmp[pl.ds(256 + head, HEAD), :]
        for h in (0, 1):
            cols = slice(h * CHUNK, (h + 1) * CHUNK)
            kvt[chunk_of[h], g * 64:g * 64 + 32, :] = a[:, cols].astype(BF16)
            kvt[chunk_of[h], g * 64 + 32:g * 64 + 64, :] = b[:, cols].astype(BF16)
            kvt[chunk_of[h], 128 + g * 64:192 + g * 64, :] = v[:, cols].astype(BF16)
    kv_copies = []
    for h in (0, 1):
        for d in (1, 2, 3):
            block = kvt.at[chunk_of[h]]
            kv_copies.append(send(block, block, acts, 16 + h * 4 + d, me.by_quarter(d)))
    for c in kv_copies:
        c.start()
    for n in (0, 1):
        q = dot_plain(h1[...], wq[:, n * 256:(n + 1) * 256]).T
        for hd in range(4):
            base = hd * HEAD
            a, b = rope_rows(q[base:base + 32], q[base + 32:base + 64], cosine, sine)
            qt[n * 256 + base:n * 256 + base + 32, :] = (a * 0.125).astype(BF16)
            qt[n * 256 + base + 32:n * 256 + base + 64, :] = (b * 0.125).astype(BF16)
    ring_cot.turn()
    spreads[1].cross()
    for c in kv_copies:
        c.wait()

    def key_rows(j, carry):
        for g in (0, 1):
            kr[j, g] = kvt[j, g * 64:(g + 1) * 64, :].astype(F32).T.astype(BF16)
        return carry

    lax.fori_loop(0, 8, key_rows, 0)

    def attend_begin():
        mx[...] = jnp.full(mx.shape, -1e30, F32)
        sm[...] = jnp.zeros(sm.shape, F32)
        acc[...] = jnp.zeros(acc.shape, F32)

    def attend(h, low, high):
        cols = slice(h * CHUNK, (h + 1) * CHUNK)

        def step(j, carry):
            at = lax.broadcasted_iota(jnp.int32, (CHUNK, CHUNK), 0) + j * CHUNK
            ok = (at >= starts[h]) & (at <= places[h])
            for hd in range(8):
                g = hd // 4
                s = jnp.where(ok, dot_plain(kr[j, g], qt[hd * 64:(hd + 1) * 64, cols]), -1e30)
                old = mx[hd:hd + 1, :]
                new = jnp.maximum(old, jnp.max(s, 0, keepdims=True))
                p = jnp.exp(s - new)
                shrink = jnp.exp(old - new)
                mx[hd:hd + 1, :] = new
                sm[hd:hd + 1, :] = sm[hd:hd + 1, :] * shrink + jnp.sum(p, 0, keepdims=True)
                acc[hd * 64:(hd + 1) * 64, :] = acc[hd * 64:(hd + 1) * 64, :] * shrink + dot_plain(
                    kvt[j, 128 + g * 64:192 + g * 64, :], p.astype(BF16)
                )
            return carry

        lax.fori_loop(low, high, step, 0)

    def attend_end(h):
        cols = slice(h * CHUNK, (h + 1) * CHUNK)
        lse[h] = mx[...] + jnp.log(sm[...])
        for hd in range(8):
            rows = slice(hd * 64, (hd + 1) * 64)
            acc[rows, :] = acc[rows, :] / sm[hd:hd + 1, :]
        ot[:, cols] = acc[...].astype(BF16)
        o_r[cols, :] = acc[...].T.astype(BF16)

    def project(h):
        rows = slice(h * CHUNK, (h + 1) * CHUNK)

        def step(n, carry):
            cols = lanes(n * 256, 256)
            part[rows, cols] = dot_plain(o_r[rows, :], wo[:, cols]).astype(BF16)
            return carry

        lax.fori_loop(0, 8, step, 0)

    sums = [RingSum(me, part, pl.ds(h * CHUNK, CHUNK), hop.at[h], got.at[h], acts, 24 + 6 * h) for h in (0, 1)]
    rings = [Ring(me, mf, pl.ds(h * CHUNK, CHUNK), acts, 36 + 4 * h) for h in (0, 1)]
    own = lanes(x * 512, 512)

    def stream(h):
        rows = pl.ds(h * CHUNK, CHUNK)
        total = xf[rows, own].astype(F32) + sums[h].finish()
        x1[rows, :] = total
        mf[rows, own] = total.astype(BF16)

    attend_begin()
    attend(0, 0, chunk_of[0] + 1)
    attend_end(0)
    spreads[1].finish()
    project(0)
    sums[0].start()
    attend_begin()
    attend(1, 0, 3)
    sums[0].turn()
    for s in spreads[2:]:
        s.cross()
    attend(1, 3, chunk_of[1] + 1)
    attend_end(1)
    stream(0)
    rings[0].start()
    project(1)
    sums[1].start()
    rings[0].turn()
    sums[1].turn()
    stream(1)
    rings[1].start()
    ring_cot.finish()
    for s in spreads[2:]:
        s.finish()
    rings[1].turn()
    for h in (0, 1):
        rings[h].finish()
        sums[h].drain()


def forward(tok, cot, wq, wo, wg, wu, wd, w_key, w_value, gain1, ids):
    ff = wg.shape[1]
    sds = jax.ShapeDtypeStruct
    outs = [
        sds((T, 2048), BF16), sds((T, 2048), BF16), sds((T, 2048), BF16),
        sds((2048, 512), BF16), sds((512, 2048), BF16),
        sds((2, 2048, ff), BF16), sds((2, 2048, ff), BF16), sds((2, ff, 2048), BF16),
        sds((512, T), BF16), sds((8, 256, CHUNK), BF16), sds((2, 8, CHUNK), F32), sds((512, T), BF16),
        sds((T, 512), F32), sds((T, 2048), BF16), sds((T, 1), F32),
    ]
    dma = pltpu.SemaphoreType.DMA
    vm = pl.BlockSpec(memory_space=pltpu.VMEM)
    return pl.pallas_call(
        forward_kernel, out_shape=outs, in_specs=[ANY] * 7 + [vm] * 4, out_specs=[vm] * len(outs),
        scratch_shapes=[
            pltpu.VMEM((T, 2048), BF16), pltpu.VMEM((2, 2, 256, 256), BF16), pltpu.VMEM((2, 2, 256, 512), BF16),
            pltpu.VMEM((512, CHUNK), F32), pltpu.VMEM((8, CHUNK), F32), pltpu.VMEM((8, CHUNK), F32),
            pltpu.VMEM((8, 2, CHUNK, 64), BF16), pltpu.VMEM((T, 512), BF16), pltpu.VMEM((512, T), F32),
            dma((44,)), dma((44,)), dma((5, 31)), dma((5, 31)), dma((7,)),
        ],
        compiler_params=pltpu.CompilerParams(collective_id=0, has_side_effects=True, vmem_limit_bytes=60 << 20),
    )(tok, cot, wq, wo, wg, wu, wd, w_key, w_value, gain1, ids)


def quarters_kernel(mine, everyone, ss, rs, ls):
    me = Place()
    greet([me.by_quarter(i) for i in (1, 2, 3)])
    slots = (me.quarter, 7 - me.quarter)
    copies = []
    for h in (0, 1):
        for d in (1, 2, 3):
            copies.append(send(mine.at[h], everyone.at[slots[h]], (ss, rs), h * 4 + d, me.by_quarter(d)))
    local = [pltpu.make_async_copy(mine.at[h], everyone.at[slots[h]], ls.at[h]) for h in (0, 1)]
    for c in copies + local:
        c.start()
    for c in copies + local:
        c.wait()


def quarters_gather(mine, cid):
    dma = pltpu.SemaphoreType.DMA
    return pl.pallas_call(
        quarters_kernel, out_shape=jax.ShapeDtypeStruct((8,) + mine.shape[1:], mine.dtype),
        in_specs=[ANY], out_specs=ANY, scratch_shapes=[dma((8,)), dma((8,)), dma((2,))],
        compiler_params=pltpu.CompilerParams(collective_id=cid, has_side_effects=True),
    )(mine)


def quarters_back_kernel(parts, got, ss, rs):
    me = Place()
    greet([me.by_quarter(i) for i in (1, 2, 3)])
    copies = []
    for d in (1, 2, 3):
        q = (me.quarter + d) % 4
        for h, slot in ((0, q), (1, 7 - q)):
            copies.append(send(parts.at[slot], got.at[d - 1, h], (ss, rs), h * 4 + d, me.by_quarter(d)))
    for c in copies:
        c.start()
    for c in copies:
        c.wait()


def quarters_back(parts, cid):
    dma = pltpu.SemaphoreType.DMA
    return pl.pallas_call(
        quarters_back_kernel, out_shape=jax.ShapeDtypeStruct((3, 2) + parts.shape[1:], parts.dtype),
        in_specs=[ANY], out_specs=ANY, scratch_shapes=[dma((8,)), dma((8,))],
        compiler_params=pltpu.CompilerParams(collective_id=cid, has_side_effects=True),
    )(parts)


def return_kernel(pieces, home, ss, rs, ls):
    me = Place()
    greet([me.by_quarter(i) for i in (1, 2, 3)])

    def piece(q):
        half, block = q // 2, q % 2
        row = jnp.where(half == 0, me.quarter, 3 - me.quarter)
        return pieces.at[half, block], home.at[pl.ds(pl.multiple_of(row * CHUNK, CHUNK), CHUNK)]

    copies = []
    for d in (1, 2, 3):
        src, dst = piece((me.quarter + d) % 4)
        copies.append(send(src, dst, (ss, rs), d, me.by_quarter(d)))
    src, dst = piece(me.quarter)
    copies.append(pltpu.make_async_copy(src, dst, ls))
    for c in copies:
        c.start()
    for c in copies:
        c.wait()


def return_home(pieces, cid):
    dma = pltpu.SemaphoreType.DMA
    return pl.pallas_call(
        return_kernel, out_shape=jax.ShapeDtypeStruct((1024, 256), pieces.dtype),
        in_specs=[ANY], out_specs=ANY, scratch_shapes=[dma((4,)), dma((4,)), dma],
        compiler_params=pltpu.CompilerParams(collective_id=cid, has_side_effects=True),
    )(pieces)


def x_scatter_kernel(parts, got, ss, rs):
    me = Place()
    greet([me.by_x(i) for i in (1, 2, 3)])
    copies = [send(parts.at[(me.x + d) % 4], got.at[d - 1], (ss, rs), d, me.by_x(d)) for d in (1, 2, 3)]
    for c in copies:
        c.start()
    for c in copies:
        c.wait()


def x_scatter(parts, cid):
    dma = pltpu.SemaphoreType.DMA
    got = pl.pallas_call(
        x_scatter_kernel, out_shape=jax.ShapeDtypeStruct((3,) + parts.shape[1:], parts.dtype),
        in_specs=[ANY], out_specs=ANY, scratch_shapes=[dma((4,)), dma((4,))],
        compiler_params=pltpu.CompilerParams(collective_id=cid, has_side_effects=True),
    )(parts)
    own = lax.dynamic_index_in_dim(parts, lax.axis_index("col") % 4, 0, keepdims=False)
    return own.astype(F32) + jnp.sum(got.astype(F32), 0)


def x_gather_kernel(mine, full, ss, rs, ls):
    me = Place()
    greet([me.by_x(1), me.by_x(3)])
    local = pltpu.make_async_copy(mine, full.at[me.x], ls)
    local.start()
    local.wait()
    one, two = ring_gather(me, full, (ss, rs))
    for c in one:
        c.start()
    for a, b in zip(one, two):
        a.wait_recv()
        b.start()
    for a in one:
        a.wait_send()
    for b in two:
        b.wait()


def x_gather(mine, cid):
    dma = pltpu.SemaphoreType.DMA
    return pl.pallas_call(
        x_gather_kernel, out_shape=jax.ShapeDtypeStruct((4,) + mine.shape, mine.dtype),
        in_specs=[pl.BlockSpec(memory_space=pltpu.VMEM)], out_specs=ANY, scratch_shapes=[dma((4,)), dma((4,)), dma],
        compiler_params=pltpu.CompilerParams(collective_id=cid, has_side_effects=True),
    )(mine)


def core_kernel(count, *refs):
    me = Place()
    greet([me.partner()])
    parts, got, ss, rs = refs[:count], refs[count:2 * count], refs[-2], refs[-1]
    copies = [send(p.at[1 - me.core], g, (ss, rs), n, me.partner()) for n, (p, g) in enumerate(zip(parts, got))]
    for c in copies:
        c.start()
    for c in copies:
        c.wait()


def line_kernel(axes, *refs):
    me = Place()
    greet([me.by_z(i) for i in (1, 2, 3)] + [me.by_y(i) for i in (1, 2, 3)])
    count = len(axes)
    parts, got, ss, rs = refs[:count], refs[count:2 * count], refs[-2], refs[-1]
    copies = []
    for n, (p, g) in enumerate(zip(parts, got)):
        for d in (1, 2, 3):
            if axes[n] == "z":
                copies.append(send(p.at[(me.z + d) % 4], g.at[d - 1], (ss, rs), n * 4 + d, me.by_z(d)))
            else:
                copies.append(send(p.at[(me.y + d) % 4], g.at[d - 1], (ss, rs), n * 4 + d, me.by_y(d)))
    for c in copies:
        c.start()
    for c in copies:
        c.wait()


def scatter_grads(grads, first_z, cid):
    count = len(grads)
    dma = pltpu.SemaphoreType.DMA
    params = dict(in_specs=[ANY] * count, out_specs=[ANY] * count)
    me = Place()
    got = pl.pallas_call(
        functools.partial(core_kernel, count),
        out_shape=[jax.ShapeDtypeStruct(g.shape[1:], BF16) for g in grads],
        scratch_shapes=[dma((count,)), dma((count,))],
        compiler_params=pltpu.CompilerParams(collective_id=cid, has_side_effects=True), **params,
    )(*grads)
    sums = []
    for g, h, fz in zip(grads, got, first_z):
        s = lax.dynamic_index_in_dim(g, me.core, 0, keepdims=False).astype(F32) + h.astype(F32)
        s = s.astype(BF16)
        sums.append(s if fz else jnp.swapaxes(s, 0, 1))
    for step in (0, 1):
        axes = tuple("z" if fz == (step == 0) else "y" for fz in first_z)
        got = pl.pallas_call(
            functools.partial(line_kernel, axes),
            out_shape=[jax.ShapeDtypeStruct((3,) + s.shape[1:], BF16) for s in sums],
            scratch_shapes=[dma((4 * count,)), dma((4 * count,))],
            compiler_params=pltpu.CompilerParams(collective_id=cid + 1 + step, has_side_effects=True), **params,
        )(*sums)
        new = []
        for s, h, axis in zip(sums, got, axes):
            own = lax.dynamic_index_in_dim(s, me.z if axis == "z" else me.y, 0, keepdims=False)
            total = own.astype(F32) + jnp.sum(h.astype(F32), 0)
            new.append(total.astype(BF16) if step == 0 else total)
        sums = new
    return sums


def angles(positions, half):
    freq = jnp.exp(-math.log(10000.0) * jnp.arange(half, dtype=jnp.float32) / half)
    turned = positions.astype(jnp.float32)[:, None] * freq[None, :]
    return (jnp.cos(turned), jnp.sin(turned))


def rotate(values, cosine, sine, sign):
    count = values.shape[0]
    parts = values.reshape(count, -1, 2, cosine.shape[1])
    first = parts[:, :, 0]
    second = parts[:, :, 1]
    cos_b = cosine[:, None, :]
    sin_b = sine[:, None, :] * sign
    return jnp.stack([first * cos_b - second * sin_b, second * cos_b + first * sin_b], 2).reshape(
        values.shape
    )


def flat(full):
    return full.transpose(1, 0, 2).reshape(T, 2048)


def blocks(value):
    return value.reshape(T, 4, 512).transpose(1, 0, 2)


def norm_back(partial_value, rows_f, rstd, gain):
    scaled = partial_value * gain
    inner = jnp.sum(scaled * rows_f, -1, keepdims=True)
    term = rstd * scaled - rows_f * (rstd * rstd * rstd / rows_f.shape[1]) * inner
    gain_grad = jnp.sum(partial_value * rows_f * rstd, 0)
    return term, gain_grad


def by_row(value, cols):
    v = value.reshape(2, 2, 2, 2, 128, cols)
    return v.transpose(3, 2, 0, 1, 4, 5).reshape(2, 4, 2, 128, cols)


def by_row_cols(value, rows):
    v = value.reshape(rows, 2, 2, 2, 2, 128)
    return v.transpose(4, 3, 1, 2, 0, 5).reshape(2, 4, 2, rows, 128)


def to_device_order(vector):
    return vector.reshape(2, 4, 256).transpose(1, 0, 2).reshape((2048,) + vector.shape[1:])


def shards(tokens, segment_ids, norm_one, w_query, w_key, w_value, w_out, norm_two, w_gate, w_up, w_down, cotangent):
    me = Place()
    x = me.x
    ids = segment_ids.reshape(8, 16, 128)
    (xf, cf, mf, q_w, o_w, g_w, u_w, d_w, qt, kvt, lse, ot, stream, normed_one, rstd_one) = forward(
        tokens, cotangent, w_query, w_out, w_gate, w_up, w_down, w_key, w_value, norm_one.reshape(1, 2048), ids
    )

    def kv_cols(w):
        w = w.reshape(2, 4, 256, 2, 2, 64)
        w = lax.dynamic_index_in_dim(w, x // 2, 4, keepdims=False)
        return w.transpose(1, 0, 2, 3, 4).reshape(2048, 128)

    kv_w = jnp.concatenate([kv_cols(w_key), kv_cols(w_value)], 1)
    gain_one = to_device_order(norm_one.astype(F32))
    gain_two = to_device_order(norm_two.astype(F32))

    seq = me.z * 2 + me.yh
    seq_ids = lax.dynamic_slice_in_dim(segment_ids, seq * 2048, 2048).reshape(8, CHUNK)
    i = me.quarter
    chunk_at = jnp.stack([i, 7 - i])
    own_ids = jnp.concatenate([lax.dynamic_index_in_dim(seq_ids, i, 0, False), lax.dynamic_index_in_dim(seq_ids, 7 - i, 0, False)])
    place = (chunk_at[:, None] * CHUNK + jnp.arange(CHUNK, dtype=jnp.int32)[None]).reshape(T)
    seq_ids = seq_ids.reshape(2048)
    before = jnp.sum((seq_ids[None, :] < own_ids[:, None]).astype(jnp.int32), 1)
    cosine, sine = angles(place - before, HEAD // 2)
    allowed = (own_ids[:, None] == seq_ids[None, :]) & (jnp.arange(2048)[None, :] <= place[:, None])
    inputs_f = xf.astype(F32)
    queries = (qt * 8).T
    kv_all = kvt.transpose(0, 2, 1).reshape(2048, 256)

    def key_of(head):
        return kv_all[:, (head // 4) * 64:(head // 4 + 1) * 64]

    def value_of(head):
        return kv_all[:, 128 + (head // 4) * 64:128 + (head // 4 + 1) * 64]

    logs = [lse[:, head].reshape(T, 1) for head in range(8)]
    attended = ot.T
    own_tok = lax.dynamic_slice_in_dim(xf, x * 512, 512, 1).astype(F32)
    own_cot = lax.dynamic_slice_in_dim(cf, x * 512, 512, 1).astype(F32)
    middle_f = mf.astype(F32)
    cot_rows = cf
    rstd_two = lax.rsqrt(jnp.mean(middle_f * middle_f, -1, keepdims=True) + eps)
    normed_two = (middle_f * rstd_two * gain_two).astype(BF16)

    feed = 0.0
    d_normed_two = 0.0
    g_gate, g_up, g_down = [], [], []
    for b in (0, 1):
        gate = dot_plain(normed_two, g_w[b])
        up = dot_plain(normed_two, u_w[b])
        sigma = jax.nn.sigmoid(gate)
        active = gate * sigma
        hidden = (active * up).astype(BF16)
        feed = feed + dot_plain(hidden, d_w[b])
        d_hidden = dot_nt(cot_rows, d_w[b])
        g_down.append(dot_tn(hidden, cot_rows).astype(BF16))
        d_gate = (d_hidden * up * sigma * (1.0 + gate * (1.0 - sigma))).astype(BF16)
        d_up = (d_hidden * active).astype(BF16)
        g_gate.append(dot_tn(normed_two, d_gate).astype(BF16))
        g_up.append(dot_tn(normed_two, d_up).astype(BF16))
        d_normed_two = d_normed_two + dot_nt(d_gate, g_w[b]) + dot_nt(d_up, u_w[b])
    result = stream + x_scatter(blocks(feed.astype(BF16)), 4)
    mixed = return_home(result.astype(BF16).reshape(2, CHUNK, 2, 256).transpose(0, 2, 1, 3), 5)
    term_two, gain_two_grad = norm_back(d_normed_two, middle_f, rstd_two, gain_two)
    d_stream = own_cot + x_scatter(blocks(term_two.astype(BF16)), 6)
    d_rows = flat(x_gather(d_stream.astype(BF16), 7))
    d_attended = dot_nt(d_rows, o_w).astype(BF16)
    g_out = dot_tn(attended, d_rows).astype(BF16)

    dq_list, dk_list, dv_list = [], [0.0, 0.0], [0.0, 0.0]
    for head in range(8):
        qh = queries[:, head * HEAD:(head + 1) * HEAD]
        gh = d_attended[:, head * HEAD:(head + 1) * HEAD]
        s = jnp.where(allowed, dot_nt(qh, key_of(head)) * 0.125, -1e30)
        p = jnp.where(allowed, jnp.exp(s - logs[head]), 0.0)
        dp = dot_nt(gh, value_of(head))
        delta = jnp.sum(p * dp, 1, keepdims=True)
        ds = (p * (dp - delta) * 0.125).astype(BF16)
        dq_list.append(dot_plain(ds, key_of(head)))
        dk_list[head // 4] = dk_list[head // 4] + dot_tn(ds, qh)
        dv_list[head // 4] = dv_list[head // 4] + dot_tn(p.astype(BF16), gh)
    dkv = jnp.concatenate(dk_list + dv_list, 1).reshape(8, CHUNK, 256)
    got = quarters_back(dkv.astype(BF16), 8)
    own = jnp.stack([lax.dynamic_index_in_dim(dkv, i, 0, False), lax.dynamic_index_in_dim(dkv, 7 - i, 0, False)])
    dkv = (own + jnp.sum(got.astype(F32), 0)).reshape(T, 256)
    dq_pre = rotate(jnp.concatenate(dq_list, 1), cosine, sine, -1.0).astype(BF16)
    dkv_pre = jnp.concatenate([rotate(dkv[:, :128], cosine, sine, -1.0), dkv[:, 128:]], 1).astype(BF16)
    g_query = dot_tn(normed_one, dq_pre).astype(BF16)
    g_kv = dot_tn(normed_one, dkv_pre).astype(BF16)
    d_normed_one = dot_nt(dq_pre, q_w) + dot_nt(dkv_pre, kv_w)
    term_one, gain_one_grad = norm_back(d_normed_one, inputs_f, rstd_one, gain_one)
    d_tokens = d_stream + x_scatter(blocks(term_one.astype(BF16)), 9)
    input_grad = return_home(d_tokens.reshape(2, CHUNK, 2, 256).transpose(0, 2, 1, 3), 10)

    def with_y(v):
        return v.reshape((2, 4, 4) + v.shape[4:])

    gq = with_y(by_row(g_query, 512).reshape(2, 4, 2, 128, 2, 256).transpose(0, 1, 2, 4, 3, 5))
    go = with_y(by_row_cols(g_out, 512).reshape(2, 4, 2, 2, 256, 128))
    ff = w_gate.shape[1]
    gg, gu = [with_y(jnp.stack([by_row(v, ff) for v in gs], 3)) for gs in (g_gate, g_up)]
    gd = with_y(jnp.stack([by_row_cols(v, ff) for v in g_down], 3))
    gkv = with_y(by_row(g_kv, 256).reshape(2, 4, 2, 2, 64, 256))
    query_s, out_s, gate_s, up_s, down_s, kv_s = scatter_grads(
        [gq, go, gg, gu, gd, gkv], (True, True, True, False, False, True), 11
    )
    shape = (2048, 256)
    pos = ((me.z // 2) * 4 + (me.z % 2) * 2 + me.yh) * 256 + me.core * 128 + me.yl * 64
    empty = jnp.zeros((2048, 4, 64), F32)
    kv_s = kv_s.reshape(64, 4, 64)

    def spread(pair):
        part = lax.dynamic_update_slice(jnp.zeros((64, 4, 64), F32), pair[:, 0:1], (0, x // 2, 0))
        part = lax.dynamic_update_slice(part, pair[:, 1:2], (0, 2 + x // 2, 0))
        return lax.dynamic_update_slice(empty, part, (pos, 0, 0)).reshape(shape)

    stats = jnp.stack([jnp.sum(own_tok * own_tok), jnp.sum(stream * stream), jnp.sum(result * result)])
    key_total, value_total = lax.psum((spread(kv_s[:, :2]), spread(kv_s[:, 2:])), ("row", "col"))
    one_total, two_total, stat_total = lax.psum((gain_one_grad, gain_two_grad, stats), ("row", "col"))

    def from_device_order(v):
        return v.reshape(4, 2, 256).transpose(1, 0, 2).reshape(2048)

    rms = jnp.sqrt(stat_total / (16384 * 2048))
    return (
        mixed, input_grad, query_s, key_total, value_total, out_s, gate_s, up_s, down_s,
        from_device_order(one_total), from_device_order(two_total), rms,
    )


def solution(mesh):
    return jax.shard_map(
        shards,
        mesh=mesh,
        in_specs=(
            P("row", "col"), P(), P(), P("row", "col"), P(), P(), P("col", "row"), P(),
            P("row", "col"), P("row", "col"), P("col", "row"), P("row", "col"),
        ),
        out_specs=(
            P("row", "col"), P("row", "col"), P("row", "col"), P(), P(), P("col", "row"),
            P("row", "col"), P("row", "col"), P("col", "row"), P(), P(), P(),
        ),
        check_vma=False,
    )
```

profile of v0, /device:TPU:1, one launch (start us, length us, event | category | flops | bytes accessed | tf_op | source)
XLA Modules:
  0.0 950.3 jit_solution(708449199361112549)
XLA Ops:
  13.4 170.7 %shard_map.211 = (bf16[512,2048]{1,0:T(8,128)(2,1)}, bf16[512,2048]{1,0:T(8,128)(2,1)}, bf16[512,2048]{1,0:T(8,128)(2,1)}, bf16[2048,512]{1,0:T(8,128)(2,1)}, bf...) custom-call(bf16[1024,256]{1,0:T(8,128)(2,1)} %tok.1, ...), custom_call_target="tpu_custom_call" | custom-call | tf_op jit(solution)/shard_map/pallas_call | solution.py:520
  186.2 4.5 fusion.29
  227.8 4.7 convolution_convert_fusion.3
  232.5 7.0 fusion.17
  247.0 25.0 %shard_map.214 = bf16[3,512,512]{2,1,0:T(8,128)(2,1)} custom-call(bf16[4,512,512]{2,1,0:T(8,128)(2,1)} %bitcast.305), custom_call_target="tpu_custom_call" | custom-call | tf_op jit(solution)/shard_map/pallas_call | solution.py:621
  276.4 22.3 %shard_map.215 = bf16[4,512,512]{2,1,0:T(8,128)(2,1)} custom-call(bf16[512,512]{1,0:T(8,128)(2,1)} %fusion.99.mine), custom_call_target="tpu_custom_call" | custom-call | tf_op jit(solution)/shard_map/pallas_call | solution.py:650
  388.1 21.8 %shard_map.216 = bf16[3,2,256,256]{3,2,1,0:T(8,128)(2,1)} custom-call(bf16[8,256,256]{2,1,0:T(8,128)(2,1)} %convert_element_type.414.parts), custom_call_target="tpu_custom_call" | custom-call | tf_op jit(solution)/shard_map/pallas_call | solution.py:572
  412.9 7.7 reshape.366
  420.6 8.7 copy.163
  429.3 7.7 reshape.369
  437.0 8.7 copy.165
  445.7 5.0 convolution_convert_fusion.4
  450.7 7.7 reshape.372
  462.5 7.7 reshape.365
  470.3 8.6 copy.162
  478.8 7.7 reshape.368
  486.6 9.0 copy.164
  495.6 5.1 convolution_convert_fusion.5
  500.6 7.7 reshape.371
  563.6 5.1 pad_maximum_fusion
  568.7 18.7 %shard_map.219 = (bf16[4,4,128,256]{3,2,1,0:T(8,128)(2,1)}, bf16[4,4,256,128]{3,2,1,0:T(8,128)(2,1)}, bf16[4,4,128,704]{3,2,1,0:T(8,128)(2,1)}, bf16[4,4,128,704...) custom-call(bf16[2,4,4,128,256]{4,3,2,1,0:T(8,128)(2,1)} %bitcast.308, ...), custom_call_target="tpu_custom_call" | custom-call | tf_op jit(solution)/shard_map/pallas_call | solution.py:691
  589.6 5.1 fusion.2
  604.4 70.8 %shard_map.220 = (bf16[3,4,128,256]{3,2,1,0:T(8,128)(2,1)}, bf16[3,4,256,128]{3,2,1,0:T(8,128)(2,1)}, bf16[3,4,128,704]{3,2,1,0:T(8,128)(2,1)}, bf16[3,4,128,704...) custom-call(bf16[4,4,128,256]{3,2,1,0:T(8,128)(2,1)} %fusion.57.refs_0_, ...), custom_call_target="tpu_custom_call" | custom-call | tf_op jit(solution)/shard_map/pallas_call | solution.py:704
  690.4 19.4 %shard_map.221 = (bf16[3,128,256]{2,1,0:T(8,128)(2,1)}, bf16[3,256,128]{2,1,0:T(8,128)(2,1)}, bf16[3,128,704]{2,1,0:T(8,128)(2,1)}, bf16[3,128,704]{2,1,0:T(8,12...) custom-call(bf16[4,128,256]{2,1,0:T(8,128)(2,1)} %fusion.82.refs_0_, ...), custom_call_target="tpu_custom_call" | custom-call | tf_op jit(solution)/shard_map/pallas_call | solution.py:704
  718.9 5.8 fusion.40
  730.0 6.6 add_convert_fusion
  741.8 27.0 %shard_map.212 = bf16[3,512,512]{2,1,0:T(8,128)(2,1)} custom-call(bf16[4,512,512]{2,1,0:T(8,128)(2,1)} %bitcast.322), custom_call_target="tpu_custom_call" | custom-call | tf_op jit(solution)/shard_map/pallas_call | solution.py:621
  785.1 27.8 %shard_map.217 = bf16[3,512,512]{2,1,0:T(8,128)(2,1)} custom-call(bf16[4,512,512]{2,1,0:T(8,128)(2,1)} %bitcast.323), custom_call_target="tpu_custom_call" | custom-call | tf_op jit(solution)/shard_map/pallas_call | solution.py:621
  814.7 4.5 multiply_reduce_fusion.9
  825.8 10.2 %shard_map.213 = bf16[1024,256]{1,0:T(8,128)(2,1)} custom-call(bf16[2,2,256,256]{3,2,1,0:T(8,128)(2,1)} %bitcast.343), custom_call_target="tpu_custom_call" | custom-call | tf_op jit(solution)/shard_map/pallas_call | solution.py:602
  840.1 14.7 %shard_map.218 = f32[1024,256]{1,0:T(8,128)} custom-call(f32[2,2,256,256]{3,2,1,0:T(8,128)} %bitcast.335), custom_call_target="tpu_custom_call" | custom-call | tf_op jit(solution)/shard_map/pallas_call | solution.py:602
  861.5 65.5 %all-reduce = (f32[2048]{0:T(1024)}, f32[2048]{0:T(1024)}, f32[3]{0:T(128)S(1)}) all-reduce(f32[2048]{0:T(1024)S(1)} %bitcast.372, f32[2048]{0:T(1024)S(1)} %bitcast.371, f32[3]{0:T(128)S(1)} %pad_maximum_fusion.9), channel_id=1, replica_groups=mesh['row'=16,'col'=8] {'row','col'}, use_global_device_ids=true, to_apply=%region_31.32 | all-reduce | flops 4099 | bytes 32792 | tf_op jit(solution)/shard_map/psum | solution.py:887
  (358 shorter events, 305.8 us)
Async XLA Ops:
  7.2 928.2 %all-reduce.4.cloned.1.call-start = ((), (), s32[]{:S(2)}) async-start(), calls=%async_computation | async-start | bytes 8388608 | tf_op jit(solution)/shard_map/psum | solution.py:886
  186.1 5.0 copy-start.68
  186.1 6.9 slice-start.4
  227.8 4.7 copy-start.40
  273.8 29.2 %copy-start.32 = (f32[512,512]{1,0:T(8,128)}, f32[512,512]{1,0:T(8,128)S(1)}, u32[]{:S(2)}) copy-start(f32[512,512]{1,0:T(8,128)S(1)} %convert_reduce_fusion.5) | copy-start | bytes 3145732
  306.5 27.8 %copy-start.47 = (bf16[512,512]{0,1:T(8,128)(2,1)}, bf16[512,512]{0,1:T(8,128)(2,1)S(1)}, u32[]{:S(2)}) copy-start(bf16[512,512]{0,1:T(8,128)(2,1)S(1)} %convolution_convert_fusion.9) | copy-start | bytes 1572868
  323.0 6.9 copy-start.66
  323.0 7.0 copy-start.61
  347.1 29.4 %copy-start.3 = (bf16[512,2048]{1,0:T(8,128)(2,1)}, bf16[512,2048]{1,0:T(8,128)(2,1)S(1)}, u32[]{:S(2)}) copy-start(bf16[512,2048]{1,0:T(8,128)(2,1)S(1)} %multiply_convert_fusion.5) | copy-start | bytes 6291460
  352.7 24.4 %copy-start.5 = (bf16[512,2048]{1,0:T(8,128)(2,1)}, bf16[512,2048]{1,0:T(8,128)(2,1)S(1)}, u32[]{:S(2)}) copy-start(bf16[512,2048]{1,0:T(8,128)(2,1)S(1)} %multiply_convert_fusion.4) | copy-start | bytes 6291460
  364.2 13.4 %copy-start.9 = (bf16[512,2048]{1,0:T(8,128)(2,1)}, bf16[512,2048]{1,0:T(8,128)(2,1)S(1)}, u32[]{:S(2)}) copy-start(bf16[512,2048]{1,0:T(8,128)(2,1)S(1)} %multiply_convert_fusion.2) | copy-start | bytes 6291460
  369.9 8.2 copy-start.11
  519.7 5.1 copy-start.4
  519.7 6.5 copy-start.6
  527.6 4.8 copy-start.14
  529.2 4.8 copy-start.62
  529.2 5.1 copy-start.67
  550.2 5.7 copy-start.2
  550.2 5.7 copy-start.27
  550.2 6.8 copy-start.28
  568.7 18.7 %copy-start.36 = (bf16[2,2,2,2,128,256]{5,4,1,0,2,3:T(8,128)(2,1)S(1)}, bf16[2,2,2,2,128,256]{5,4,1,0,2,3:T(8,128)(2,1)}, u32[]{:S(2)}) copy-start(bf16[2,2,2,2,128,256]{5,4,1,0,2,3:T(8,128)(2,1)} %copy.168) | copy-start | bytes 3145732
  587.4 7.3 copy-start.43
  589.6 5.1 copy-start.1
  589.6 7.8 slice-start
  675.2 5.4 copy-start.56
  675.2 7.4 copy-start.46
  711.6 4.9 copy-start.65
  711.6 4.9 copy-start.39
  785.1 29.6 %copy-start.33 = (f32[512,512]{1,0:T(8,128)S(1)}, f32[512,512]{1,0:T(8,128)}, u32[]{:S(2)}) copy-start(f32[512,512]{1,0:T(8,128)} %copy-done.32) | copy-start | bytes 3145732
  819.2 16.8 %copy-start.37 = (f32[512,512]{1,0:T(8,128)S(1)}, f32[512,512]{1,0:T(8,128)}, u32[]{:S(2)}) copy-start(f32[512,512]{1,0:T(8,128)} %get-tuple-element.186) | copy-start | bytes 3145732
  837.7 18.9 %copy-start.58 = (bf16[3,128,704]{2,1,0:T(8,128)(2,1)S(1)}, bf16[3,128,704]{2,1,0:T(8,128)(2,1)}, u32[]{:S(2)}) copy-start(bf16[3,128,704]{2,1,0:T(8,128)(2,1)} %get-tuple-element.76) | copy-start | bytes 1622020
  935.3 6.7 copy-start.38
  (45 other events, 148.7 us)
Sparse Core Ops, SparseCore 0:
  716.6 185.4 all-reduce.3
where the time goes:
time: 961 us; the launch traced here: 950 us
  Pallas kernels  428 us (45%)
  local copies, waits for them, and re-layouts  204 us (21%)
  matrix products  150 us (16%)
  other arithmetic  86.3 us (9%)
  blocking collectives  65.5 us (7%)
  between operations  16 us (2%)
    pallas_call x1, Pallas kernels, forward(): pl.pallas_call(forward_kernel, out_shape=outs, in_specs=[ANY] * 7 + [vm]...  171 us
    pallas_call x2, Pallas kernels, scatter_grads(): pl.pallas_call(functools.partial(line_kernel, axes), out_shape=[jax.Shape...  90.2 us
    pallas_call x3, Pallas kernels, x_scatter(): pl.pallas_call(x_scatter_kernel, out_shape=jax.ShapeDtypeStruct((3,) + pa...  79.8 us
    dot_general x25, matrix products, dot_nt(): lax.dot_general(left, right, (((1,), (1,)), ((), ())), preferred_element_...  69.8 us
    psum x1, blocking collectives, shards(): lax.psum((gain_one_grad, gain_two_grad, stats), ('row', 'col'))  65.5 us
    unnamed x169, local copies, waits for them, and re-layouts  43.9 us
    dot_general x25, matrix products, dot_tn(): lax.dot_general(left, right, (((0,), (0,)), ((), ())), preferred_element_...  42.1 us
    dot_general x14, matrix products, dot_plain(): return jnp.dot(left, right, preferred_element_type=F32)  37.8 us
  transfers between devices with their start and end apart: 1, of which 0 were waited for; matrix products, arithmetic and copies ran while one was open for 8% of the time, Pallas kernels for 8%

commit v1 on v0

v1 whole, which is shorter than its diff:
```python
import functools
import math

import jax
import jax.numpy as jnp
from jax import lax
from jax.experimental import pallas as pl
from jax.experimental.pallas import tpu as pltpu
from jax.sharding import PartitionSpec as P

BF16 = jnp.bfloat16
F32 = jnp.float32
HEAD = 64
eps = 1e-05
MESH = pl.DeviceIdType.MESH
ANY = pl.BlockSpec(memory_space=pl.ANY)
CHUNK = 256
T = 512


class Place:
    def __init__(self):
        row = lax.axis_index("row")
        col = lax.axis_index("col")
        self.z = row // 4
        self.yh = (row // 2) % 2
        self.core = row % 2
        self.yl = col // 4
        self.x = col % 4
        self.y = self.yh * 2 + self.yl
        self.quarter = self.core * 2 + self.yl

    def at(self, z, y, core, x):
        return {"row": z * 4 + (y // 2) * 2 + core, "col": (y % 2) * 4 + x}

    def by_x(self, d):
        return self.at(self.z, self.y, self.core, (self.x + d) % 4)

    def by_z(self, d):
        return self.at((self.z + d) % 4, self.y, self.core, self.x)

    def by_y(self, d):
        return self.at(self.z, (self.y + d) % 4, self.core, self.x)

    def partner(self):
        return self.at(self.z, self.y, 1 - self.core, self.x)

    def by_quarter(self, d):
        q = (self.quarter + d) % 4
        return self.at(self.z, self.yh * 2 + q % 2, q // 2, self.x)


def greet(peers):
    barrier = pltpu.get_barrier_semaphore()
    for peer in peers:
        pl.semaphore_signal(barrier, inc=1, device_id=peer, device_id_type=MESH)
    pl.semaphore_wait(barrier, len(peers))


def send(src, dst, sems, k, peer):
    return pltpu.make_async_remote_copy(
        src_ref=src, dst_ref=dst, send_sem=sems[0].at[k], recv_sem=sems[1].at[k],
        device_id=peer, device_id_type=MESH,
    )


def each(count, act):
    def step(i, carry):
        act(i)
        return carry

    lax.fori_loop(0, count, step, 0)


def perm_row(z, y, core):
    yh = y // 2
    return ((z % 2) * 2 + yh) * 512 + (z // 2) * 256 + core * 128


def reshard_in(me, src, full, sems, base, lsem):
    def chunk(q):
        return src.at[pl.ds(pl.multiple_of(jnp.where(me.core == 0, q, 3 - q) * CHUNK, CHUNK), CHUNK)]

    half = pl.multiple_of(me.core * CHUNK, CHUNK)
    place = full.at[pl.ds(half, CHUNK), pl.ds(pl.multiple_of(me.x * 512 + me.yl * 256, 256), 256)]
    copies = []
    for d in (1, 2, 3):
        copies.append(send(chunk((me.quarter + d) % 4), place, sems, base + d, me.by_quarter(d)))
    local = pltpu.make_async_copy(chunk(me.quarter), place, lsem)
    return copies, local


class Spread:
    def __init__(self, me, src, slot, z_first, sems, lsem):
        self.me, self.src, self.slot, self.z_first, self.sems, self.lsem = me, src, slot, z_first, sems, lsem

    def local(self):
        me = self.me
        return pltpu.make_async_copy(self.src, self.slot(me.z, me.y, me.core), self.lsem)

    def first(self, i):
        me = self.me
        peer = me.by_z(i + 1) if self.z_first else me.by_y(i + 1)
        return send(self.src, self.slot(me.z, me.y, me.core), self.sems, i, peer)

    def line(self, k):
        me = self.me
        if self.z_first:
            return self.slot((me.z + 4 - k) % 4, me.y, me.core)
        return self.slot(me.z, (me.y + 4 - k) % 4, me.core)

    def second(self, k, i):
        me = self.me
        peer = me.by_y(i + 1) if self.z_first else me.by_z(i + 1)
        block = self.line(k)
        return send(block, block, self.sems, 3 + k * 3 + i, peer)

    def third(self, i):
        me = self.me
        if self.z_first:
            block = self.slot((me.z + 4 - i // 4) % 4, (me.y + 4 - i % 4) % 4, me.core)
        else:
            block = self.slot((me.z + 4 - i % 4) % 4, (me.y + 4 - i // 4) % 4, me.core)
        return send(block, block, self.sems, 15 + i, me.partner())

    def start(self):
        self.local().start()
        each(3, lambda i: self.first(i).start())

    def turn(self):
        self.local().wait()
        each(3, lambda i: self.second(0, i).start())
        self.third(0).start()

        def arrived(k):
            self.first(k).wait_recv()
            each(3, lambda i: self.second(k + 1, i).start())
            self.third((k + 1) * 4).start()

        each(3, arrived)

    def cross(self):
        def arrived(j):
            k, i = j // 3, j % 3
            self.second(k, i).wait_recv()
            self.third(k * 4 + i + 1).start()

        each(12, arrived)

    def finish(self):
        each(16, lambda i: self.third(i).wait_recv())
        each(3, lambda i: self.first(i).wait_send())
        each(12, lambda j: self.second(j // 3, j % 3).wait_send())
        each(16, lambda i: self.third(i).wait_send())


def weight_slots(q, o, g, u, d):
    def ds(start, size):
        return pl.ds(pl.multiple_of(start, 128), size)

    return (
        lambda z, y, c: q.at[ds(perm_row(z, y, c), 128), ds((y % 2) * 256, 256)],
        lambda z, y, c: o.at[ds((y % 2) * 256, 256), ds(perm_row(z, y, c), 128)],
        lambda z, y, c: g.at[y % 2, ds(perm_row(z, y, c), 128)],
        lambda z, y, c: u.at[y % 2, ds(perm_row(z, y, c), 128)],
        lambda z, y, c: d.at[y % 2, :, ds(perm_row(z, y, c), 128)],
    )


def dot_plain(left, right):
    return jnp.dot(left, right, preferred_element_type=F32)


def dot_tn(left, right):
    return lax.dot_general(left, right, (((0,), (0,)), ((), ())), preferred_element_type=F32)


def dot_nt(left, right):
    return lax.dot_general(left, right, (((1,), (1,)), ((), ())), preferred_element_type=F32)


def lanes(start, size):
    return pl.ds(pl.multiple_of(start, 128), size)


class Ring:
    def __init__(self, me, full, rows, sems, base):
        x = me.x
        right, left = me.by_x(1), me.by_x(3)
        xl, xr = (x + 3) % 4, (x + 1) % 4

        def at(b, off, size):
            return full.at[rows, lanes(b * 512 + off, size)]

        self.one = [
            send(at(x, 0, 512), at(x, 0, 512), sems, base + 0, right),
            send(at(x, 0, 512), at(x, 0, 512), sems, base + 1, left),
        ]
        self.two = [
            send(at(xl, 0, 256), at(xl, 0, 256), sems, base + 2, right),
            send(at(xr, 256, 256), at(xr, 256, 256), sems, base + 3, left),
        ]

    def start(self):
        for c in self.one:
            c.start()

    def turn(self):
        for a, b in zip(self.one, self.two):
            a.wait_recv()
            b.start()

    def finish(self):
        for a in self.one:
            a.wait_send()
        for b in self.two:
            b.wait()


class RingSum:
    def __init__(self, me, part, rows, hop, got, sems, base):
        x = me.x
        self.part, self.rows, self.hop, self.got, self.x = part, rows, hop, got, x
        right, left = me.by_x(1), me.by_x(3)
        far, xr, xl = (x + 2) % 4, (x + 1) % 4, (x + 3) % 4
        self.xr, self.xl = xr, xl

        def at(b, off):
            return part.at[rows, lanes(b * 512 + off, 256)]

        self.one = [
            send(at(far, 0), hop.at[0], sems, base + 0, right),
            send(at(far, 256), hop.at[1], sems, base + 1, left),
            send(at(xr, 256), got.at[0, :, pl.ds(256, 256)], sems, base + 2, right),
            send(at(xl, 0), got.at[1, :, pl.ds(0, 256)], sems, base + 3, left),
        ]
        self.two = [
            send(at(xr, 0), got.at[0, :, pl.ds(0, 256)], sems, base + 4, right),
            send(at(xl, 256), got.at[1, :, pl.ds(256, 256)], sems, base + 5, left),
        ]

    def start(self):
        for c in self.one:
            c.start()

    def turn(self):
        for k, (b, off) in enumerate(((self.xr, 0), (self.xl, 256))):
            self.one[k].wait_recv()
            cols = lanes(b * 512 + off, 256)
            total = self.part[self.rows, cols].astype(F32) + self.hop[k].astype(F32)
            self.part[self.rows, cols] = total.astype(BF16)
            self.two[k].start()

    def finish(self):
        for k in (2, 3):
            self.one[k].wait_recv()
        for c in self.two:
            c.wait_recv()
        own = self.part[self.rows, lanes(self.x * 512, 512)].astype(F32)
        return own + self.got[0].astype(F32) + self.got[1].astype(F32)

    def drain(self):
        for c in self.one + self.two:
            c.wait_send()


def rope_rows(a, b, cosine, sine):
    return a * cosine - b * sine, b * cosine + a * sine


def document_starts(ids, seq, place):
    ids = ids[seq]

    def below(number):
        hit = (ids < number).astype(F32)
        return jnp.sum(jnp.sum(hit, 1, keepdims=True), 0, keepdims=True)

    second, third = below(3 * seq + 1).astype(jnp.int32), below(3 * seq + 2).astype(jnp.int32)
    return jnp.where(place >= third, third, jnp.where(place >= second, second, 0))


ORIGINAL = [(p % 2) * 4 + p // 2 for p in range(8)]


def device_order_row(ref):
    return jnp.concatenate([ref[:, b * 256:(b + 1) * 256].astype(F32) for b in ORIGINAL], 1)


def rms_rows(src, gain, dst, rstd, first, count):
    def step(k, carry):
        rows = pl.ds(pl.multiple_of(first + k * 64, 64), 64)
        v = src[rows, :].astype(F32)
        r = lax.rsqrt(jnp.sum(v * v, 1, keepdims=True) * (1.0 / 2048.0) + eps)
        rstd[rows, :] = r
        dst[rows, :] = (v * r * gain).astype(BF16)
        return carry

    lax.fori_loop(0, count // 64, step, 0)


def column_squares(value):
    return jnp.sum(value * value, 0, keepdims=True)


class GradSum:
    def __init__(self, me, own, land, out, rows, halves, sems, base):
        self.me, self.own, self.land, self.out, self.rows, self.halves = me, own, land, out, rows, halves
        self.sems, self.base = sems, base

    def first(self, i):
        me = self.me
        return send(self.own((me.z + 1 + i // 2) % 4, i % 2), self.land(i), self.sems, self.base + i, me.by_z(1 + i // 2))

    def start(self):
        each(6, lambda i: self.first(i).start())

    def add(self, view, others):
        def step(k, carry):
            rows = pl.ds(pl.multiple_of(k * 64, 64), 64)
            total = view[rows, :].astype(F32)
            for other in others:
                total = total + other[rows, :].astype(F32)
            view[rows, :] = total.astype(BF16)
            return carry

        lax.fori_loop(0, self.rows // 64, step, 0)

    def sum_z(self):
        each(6, lambda i: self.first(i).wait_recv())
        for yh in (0, 1):
            self.add(self.own(self.me.z, yh), [self.land(d * 2 + yh) for d in range(3)])
        each(6, lambda i: self.first(i).wait_send())

    def second(self, yh):
        me = self.me
        to = yh * 2 + me.core
        step = (to + 4 - me.y) % 4
        slot = (step + 3) % 4
        copy = pltpu.make_async_remote_copy(
            src_ref=self.own(me.z, yh), dst_ref=self.land(slot), send_sem=self.sems[0].at[self.base + 6 + yh],
            recv_sem=self.sems[1].at[self.base + 6 + slot], device_id=me.at(me.z, to, me.core, me.x), device_id_type=MESH,
        )
        return step, copy

    def send_y(self):
        for yh in (0, 1):
            step, copy = self.second(yh)
            pl.when(step != 0)(copy.start)

    def last(self):
        me = self.me
        view = self.halves(self.own(me.z, me.yh), 1 - me.core)
        return send(view, self.out, self.sems, self.base + 9, me.partner())

    def keep(self):
        me = self.me
        return pltpu.make_async_copy(self.halves(self.own(me.z, me.yh), me.core), self.out, self.sems[0].at[self.base + 10])

    def sum_y(self):
        me = self.me

        def work():
            for slot in range(3):
                pltpu.make_async_remote_copy(
                    src_ref=self.land(slot), dst_ref=self.land(slot), send_sem=self.sems[0].at[self.base + 8],
                    recv_sem=self.sems[1].at[self.base + 6 + slot], device_id=me.partner(), device_id_type=MESH,
                ).wait_recv()
            self.add(self.own(me.z, me.yh), [self.land(slot) for slot in range(3)])
            self.last().start()
            self.keep().start()

        pl.when(me.yl == me.core)(work)

    def finish(self):
        me = self.me

        def sender():
            self.last().wait_send()
            self.keep().wait()

        pl.when(me.yl == me.core)(sender)
        pl.when(me.yl != me.core)(lambda: self.last().wait_recv())
        for yh in (0, 1):
            step, copy = self.second(yh)
            pl.when(step != 0)(copy.wait_send)


def layer_kernel(
    tok, cot, wq_s, wo_s, wg_s, wu_s, wd_s, w_key, w_value, gain1, gain2, ids,
    o_mixed, o_in, o_q, o_out, o_gate, o_up, o_down, o_kv, o_small, xs,
    xf, cf, mf, h1, h2p, cfp, wq, wo, wg, wu, wd, qt, ot, o_r, kvt, x1, dx1, part, hop, got, acc, mx, sm, lse, delta,
    hid, dg, du, hp, dhf, r1, r2, mix, gains, squares, small, small_r,
    a_s, a_r, w_s, w_r, lsem, hs,
):
    me = Place()
    x, core = me.x, me.core
    h2, kv_tmp = xf, dx1
    acts = (a_s, a_r)
    count = [0]

    def sems(n):
        count[0] += n
        assert count[0] <= ACTS
        return count[0] - n

    def shake(k, peers):
        for peer in peers:
            pl.semaphore_signal(hs.at[k], inc=1, device_id=peer, device_id_type=MESH)

    def unshake(k, peers):
        pl.semaphore_wait(hs.at[k], len(peers))

    xs_line = [me.by_x(i) for i in (1, 2, 3)]
    ys_line = [me.by_y(i) for i in (1, 2, 3)]
    zs_line = [me.by_z(i) for i in (1, 2, 3)]
    four = [me.by_quarter(i) for i in (1, 2, 3)]
    partner = me.partner()
    greet(xs_line + ys_line + zs_line + four)
    slots = weight_slots(wq, wo, wg, wu, wd)
    first_z = (True, True, True, False, False)
    spreads = [
        Spread(me, src, slots[n], first_z[n], (w_s.at[n], w_r.at[n]), lsem.at[2 + n])
        for n, src in enumerate((wq_s, wo_s, wg_s, wu_s, wd_s))
    ]
    in_copies, in_local = reshard_in(me, tok, xf, acts, sems(4), lsem.at[0])
    cot_copies, cot_local = reshard_in(me, cot, cf, acts, sems(4), lsem.at[1])
    for c in in_copies + [in_local]:
        c.start()
    for s in spreads:
        s.start()
    for c in cot_copies + [cot_local]:
        c.start()
    seq = me.z * 2 + me.yh
    chunk_of = (me.quarter, 7 - me.quarter)
    lane = lax.broadcasted_iota(jnp.int32, (1, CHUNK), 1)
    places = [c * CHUNK + lane for c in chunk_of]
    starts = [document_starts(ids, seq, p) for p in places]
    pos = jnp.concatenate([p - s for p, s in zip(places, starts)], 1).astype(F32)
    turn = lax.broadcasted_iota(jnp.int32, (32, 1), 0).astype(F32)
    angle = jnp.exp(-math.log(10000.0) * turn / 32.0) * pos
    cosine, sine = jnp.cos(angle), jnp.sin(angle)
    gains[...] = jnp.zeros(gains.shape, F32)
    squares[...] = jnp.zeros(squares.shape, F32)
    small[...] = jnp.zeros(small.shape, F32)

    for c in in_copies:
        c.wait_recv()
    in_local.wait()
    ring_tok = Ring(me, xf, pl.ds(0, T), acts, sems(4))
    ring_tok.start()
    spreads[0].turn()
    spreads[1].turn()
    for c in cot_copies:
        c.wait_recv()
    cot_local.wait()
    ring_tok.turn()
    ring_cot = Ring(me, cf, pl.ds(0, T), acts, sems(4))
    ring_cot.start()
    spreads[0].cross()
    for s in spreads[2:]:
        s.turn()
    ring_tok.finish()
    for c in in_copies + cot_copies:
        c.wait_send()
    stash = pltpu.make_async_copy(xf, xs, lsem.at[7])
    stash.start()

    rms_rows(xf, device_order_row(gain1), h1, r1, 0, T)
    spreads[0].finish()
    for n, w in enumerate((w_key, w_value)):
        total = None
        for p, b in enumerate(ORIGINAL):
            d = dot_plain(h1[:, p * 256:(p + 1) * 256], w[b * 256:(b + 1) * 256, :])
            total = d if total is None else total + d
        kv_tmp[n * 256:(n + 1) * 256, :] = total.T
    heads = [pl.multiple_of((2 * g + x // 2) * HEAD, HEAD) for g in (0, 1)]
    for g in (0, 1):
        head = heads[g]
        a, b = rope_rows(kv_tmp[pl.ds(head, 32), :], kv_tmp[pl.ds(head + 32, 32), :], cosine, sine)
        v = kv_tmp[pl.ds(256 + head, HEAD), :]
        for h in (0, 1):
            cols = slice(h * CHUNK, (h + 1) * CHUNK)
            kvt[chunk_of[h], g * 64:g * 64 + 32, :] = a[:, cols].astype(BF16)
            kvt[chunk_of[h], g * 64 + 32:g * 64 + 64, :] = b[:, cols].astype(BF16)
            kvt[chunk_of[h], 128 + g * 64:192 + g * 64, :] = v[:, cols].astype(BF16)
    kv_copies = []
    base = sems(8)
    for h in (0, 1):
        for d in (1, 2, 3):
            block = kvt.at[chunk_of[h]]
            kv_copies.append(send(block, block, acts, base + h * 4 + d, me.by_quarter(d)))
    for c in kv_copies:
        c.start()
    for n in (0, 1):
        q = dot_plain(h1[...], wq[:, n * 256:(n + 1) * 256]).T
        for hd in range(4):
            at = hd * HEAD
            a, b = rope_rows(q[at:at + 32], q[at + 32:at + 64], cosine, sine)
            qt[n * 256 + at:n * 256 + at + 32, :] = (a * 0.125).astype(BF16)
            qt[n * 256 + at + 32:n * 256 + at + 64, :] = (b * 0.125).astype(BF16)
    ring_cot.turn()
    spreads[1].cross()
    for c in kv_copies:
        c.wait()

    def row_form(block):
        return block.astype(F32).T.astype(BF16)

    def allowed(h, j):
        at = lax.broadcasted_iota(jnp.int32, (CHUNK, CHUNK), 0) + j * CHUNK
        return (at >= starts[h]) & (at <= places[h])

    def attend_begin():
        mx[...] = jnp.full(mx.shape, -1e30, F32)
        sm[...] = jnp.zeros(sm.shape, F32)
        acc[...] = jnp.zeros(acc.shape, F32)

    def attend(h, low, high):
        cols = slice(h * CHUNK, (h + 1) * CHUNK)

        def step(j, carry):
            ok = allowed(h, j)
            keys = [row_form(kvt[j, g * 64:(g + 1) * 64, :]) for g in (0, 1)]
            for hd in range(8):
                g = hd // 4
                s = jnp.where(ok, dot_plain(keys[g], qt[hd * 64:(hd + 1) * 64, cols]), -1e30)
                old = mx[hd:hd + 1, :]
                new = jnp.maximum(old, jnp.max(s, 0, keepdims=True))
                p = jnp.exp(s - new)
                shrink = jnp.exp(old - new)
                mx[hd:hd + 1, :] = new
                sm[hd:hd + 1, :] = sm[hd:hd + 1, :] * shrink + jnp.sum(p, 0, keepdims=True)
                acc[hd * 64:(hd + 1) * 64, :] = acc[hd * 64:(hd + 1) * 64, :] * shrink + dot_plain(
                    kvt[j, 128 + g * 64:192 + g * 64, :], p.astype(BF16)
                )
            return carry

        lax.fori_loop(low, high, step, 0)

    def attend_end(h):
        cols = slice(h * CHUNK, (h + 1) * CHUNK)
        lse[h] = mx[...] + jnp.log(sm[...])
        for hd in range(8):
            rows = slice(hd * 64, (hd + 1) * 64)
            acc[rows, :] = acc[rows, :] / sm[hd:hd + 1, :]
        ot[:, cols] = acc[...].astype(BF16)
        o_r[cols, :] = acc[...].T.astype(BF16)

    def rows_of(h):
        return pl.ds(h * CHUNK, CHUNK)

    def project(h):
        rows = rows_of(h)

        def step(n, carry):
            cols = lanes(n * 256, 256)
            part[rows, cols] = dot_plain(o_r[rows, :], wo[:, cols]).astype(BF16)
            return carry

        lax.fori_loop(0, 8, step, 0)

    def ring_sums():
        return [RingSum(me, part, rows_of(h), hop.at[h], got.at[h], acts, sems(6)) for h in (0, 1)]

    def rings():
        return [Ring(me, mf, rows_of(h), acts, sems(4)) for h in (0, 1)]

    sums, ring = ring_sums(), rings()
    own = lanes(x * 512, 512)

    def stream(h):
        rows = rows_of(h)
        mine = xf[rows, own].astype(F32)
        total = mine + sums[h].finish()
        squares[0:1, :] += column_squares(mine)
        squares[1:2, :] += column_squares(total)
        x1[rows, :] = total
        mf[rows, own] = total.astype(BF16)

    attend_begin()
    attend(0, 0, chunk_of[0] + 1)
    attend_end(0)
    spreads[1].finish()
    project(0)
    sums[0].start()
    attend_begin()
    attend(1, 0, 3)
    sums[0].turn()
    for s in spreads[2:]:
        s.cross()
    attend(1, 3, chunk_of[1] + 1)
    attend_end(1)
    stream(0)
    ring[0].start()
    project(1)
    sums[1].start()
    ring[0].turn()
    sums[1].turn()
    stream(1)
    ring[1].start()
    ring_cot.finish()
    cot_over = send(cf, cfp, acts, sems(1), partner)
    cot_over.start()
    stash.wait()
    ring[0].finish()

    row_two = device_order_row(gain2)
    rms_rows(mf, row_two, h2, r2, 0, CHUNK)
    for s in spreads[2:]:
        s.finish()
    ring[1].turn()

    def feed_forward(h):
        rows = rows_of(h)

        def step(b, carry):
            for at, size in ((0, 256), (256, 256), (512, 192)):
                cols = slice(at, at + size)
                gate = dot_plain(h2[rows, :], wg[b, :, cols])
                up = dot_plain(h2[rows, :], wu[b, :, cols])
                d_hidden = dot_nt(cf[rows, :], wd[b, cols, :])
                sigma = 1.0 / (1.0 + jnp.exp(-gate))
                active = gate * sigma
                hid[b, rows, cols] = (active * up).astype(BF16)
                dg[b, rows, cols] = (d_hidden * up * sigma * (1.0 + gate * (1.0 - sigma))).astype(BF16)
                du[b, rows, cols] = (d_hidden * active).astype(BF16)
            return carry

        lax.fori_loop(0, 2, step, 0)

    def norm_back(h, u_ref, rstd, gain, k):
        def step(i, carry):
            at = pl.multiple_of(i * 64, 64)
            full = pl.ds(pl.multiple_of(h * CHUNK + i * 64, 64), 64)
            d = dhf[pl.ds(at, 64), :]
            u = u_ref[full, :].astype(F32)
            r = rstd[full, :]
            scaled = d * gain
            inner = jnp.sum(scaled * u, 1, keepdims=True)
            part[full, :] = (r * scaled - u * (r * r * r * (1.0 / 2048.0) * inner)).astype(BF16)
            gains[k:k + 1, :] += jnp.sum(d * u * r, 0, keepdims=True)
            return carry

        lax.fori_loop(0, CHUNK // 64, step, 0)

    def back_two(h):
        rows = rows_of(h)

        def step(n, carry):
            feats = lanes(n * 256, 256)
            total = dot_nt(dg[0, rows, :], wg[0, feats, :]) + dot_nt(dg[1, rows, :], wg[1, feats, :])
            total = total + dot_nt(du[0, rows, :], wu[0, feats, :]) + dot_nt(du[1, rows, :], wu[1, feats, :])
            dhf[:, feats] = total
            return carry

        lax.fori_loop(0, 8, step, 0)
        norm_back(h, mf, r2, row_two, 1)

    feed_forward(0)
    back_two_sums, ring_two = ring_sums(), rings()
    ring[1].finish()
    sums[0].drain()
    back_two(0)
    back_two_sums[0].start()
    rms_rows(mf, row_two, h2, r2, CHUNK, CHUNK)
    feed_forward(1)
    h2_over = send(h2, h2p, acts, sems(1), partner)
    h2_over.start()
    base = sems(3)
    hid_over = [send(ref.at[1 - core], hp.at[n], acts, base + n, partner) for n, ref in enumerate((hid, dg, du))]
    for c in hid_over:
        c.start()
    back_two_sums[0].turn()
    sums[1].drain()
    back_two(1)
    back_two_sums[1].start()

    def d_stream(h):
        rows = rows_of(h)
        total = cf[rows, own].astype(F32) + back_two_sums[h].finish()
        dx1[rows, :] = total
        mf[rows, own] = total.astype(BF16)

    d_stream(0)
    ring_two[0].start()
    h2_over.wait()
    for c in hid_over:
        c.wait()
    cot_over.wait()

    def feed(h):
        rows = rows_of(h)

        def step(n, carry):
            cols = lanes(n * 256, 256)
            part[rows, cols] = (dot_plain(hid[0, rows, :], wd[0, :, cols]) + dot_plain(hid[1, rows, :], wd[1, :, cols])).astype(BF16)
            return carry

        lax.fori_loop(0, 8, step, 0)

    def grads_in(low, high):
        def step(m, carry):
            feats = lanes(m * 256, 256)
            mine = h2[:, feats].T
            other = h2p[:, feats].T
            wg[core, feats, :] = (dot_plain(mine, dg[core]) + dot_plain(other, hp[1])).astype(BF16)
            wu[core, feats, :] = (dot_plain(mine, du[core]) + dot_plain(other, hp[2])).astype(BF16)
            return carry

        lax.fori_loop(low, high, step, 0)

    grads_in(0, 4)
    back_two_sums[1].turn()
    ring_two[0].turn()
    back_two_sums[0].drain()
    feed_sums = ring_sums()
    feed(0)
    feed_sums[0].start()
    grads_in(4, 8)
    d_stream(1)
    ring_two[1].start()
    ring_two[0].finish()
    back_two_sums[1].drain()
    ring_two[1].turn()
    feed(1)
    feed_sums[1].start()
    feed_sums[0].turn()

    for at, size in ((0, 256), (256, 256), (512, 192)):
        mine = hid[core, :, at:at + size].T
        other = hp[0, :, at:at + size].T

        def down(n, carry):
            cols = lanes(n * 512, 512)
            wd[core, at:at + size, cols] = (dot_plain(mine, cf[:, cols]) + dot_plain(other, cfp[:, cols])).astype(BF16)
            return carry

        lax.fori_loop(0, 4, down, 0)

    shake(0, zs_line + ys_line + four)
    unstash = pltpu.make_async_copy(xs, cf, lsem.at[7])
    unstash.start()

    def d_attended(h):
        cols = slice(h * CHUNK, (h + 1) * CHUNK)
        rows = rows_of(h)
        for k in (0, 1):
            feats = slice(k * 256, (k + 1) * 256)
            d = dot_nt(wo[feats, :], mf[rows, :])
            o_r[feats, cols] = d.astype(BF16)
            both = d.astype(BF16).astype(F32) * ot[feats, cols].astype(F32)
            for hd in range(4):
                delta[h, k * 4 + hd:k * 4 + hd + 1, :] = jnp.sum(both[hd * 64:(hd + 1) * 64], 0, keepdims=True)

    def attend_back(h, low, high):
        cols = slice(h * CHUNK, (h + 1) * CHUNK)

        def step(j, carry):
            ok = allowed(h, j)
            keys_at = lanes(j * CHUNK, CHUNK)
            for g in (0, 1):
                key_t = kvt[j, g * 64:(g + 1) * 64, :]
                key, value = row_form(key_t), row_form(kvt[j, 128 + g * 64:192 + g * 64, :])
                ps, ds = [], []
                for hd in range(4 * g, 4 * g + 4):
                    feats = slice(hd * 64, (hd + 1) * 64)
                    s = jnp.where(ok, dot_plain(key, qt[feats, cols]), -1e30)
                    p = jnp.exp(s - lse[h, hd:hd + 1, :])
                    dp = dot_plain(value, o_r[feats, cols])
                    d = (p * (dp - delta[h, hd:hd + 1, :])).astype(BF16)
                    acc[feats, :] += dot_plain(key_t, d)
                    ps.append(p.astype(BF16))
                    ds.append(d)
                q4 = jnp.concatenate([qt[hd * 64:(hd + 1) * 64, cols] for hd in range(4 * g, 4 * g + 4)], 1)
                do4 = jnp.concatenate([o_r[hd * 64:(hd + 1) * 64, cols] for hd in range(4 * g, 4 * g + 4)], 1)
                dhf[g * 64:(g + 1) * 64, keys_at] += dot_nt(q4, jnp.concatenate(ds, 1))
                dhf[128 + g * 64:192 + g * 64, keys_at] += dot_nt(do4, jnp.concatenate(ps, 1))
            return carry

        lax.fori_loop(low, high, step, 0)

    def attend_back_end(h):
        cols = slice(h * CHUNK, (h + 1) * CHUNK)
        for hd in range(8):
            at = hd * 64
            a, b = rope_rows(acc[at:at + 32, :] * 0.125, acc[at + 32:at + 64, :] * 0.125, cosine[:, cols], -sine[:, cols])
            acc[at:at + 32, :] = a
            acc[at + 32:at + 64, :] = b
        qt[:, cols] = acc[...].astype(BF16)
        du[0, rows_of(h), 0:512] = acc[...].T.astype(BF16)

    d_attended(0)
    dhf[...] = jnp.zeros(dhf.shape, F32)
    acc[...] = jnp.zeros(acc.shape, F32)
    feed_sums[1].turn()
    unshake(0, zs_line + ys_line + four)
    ff = wg.shape[2]
    gate_sum, up_sum = [
        GradSum(
            me, lambda z, yh, w=w: w.at[core, lanes((z % 2) * 1024 + yh * 512 + (z // 2) * 256, 256)],
            lambda i, w=w: w.at[1 - core, lanes(i * 256, 256)], out, 256, lambda v, c: v.at[lanes(c * 128, 128)], acts, sems(11),
        ) for w, out in ((wg, o_gate), (wu, o_up))
    ]
    down_sum = GradSum(
        me, lambda z, yh: wd.at[core, :, lanes((z % 2) * 1024 + yh * 512 + (z // 2) * 256, 256)],
        lambda i: wd.at[1 - core, :, lanes(i * 256, 256)], o_down, ff, lambda v, c: v.at[:, lanes(c * 128, 128)], acts, sems(11),
    )
    out_sum = GradSum(
        me, lambda z, yh: wo.at[lanes(core * 256, 256), lanes((z % 2) * 1024 + yh * 512 + (z // 2) * 256, 256)],
        lambda i: wo.at[lanes((1 - core) * 256, 256), lanes(i * 256, 256)], o_out, 256,
        lambda v, c: v.at[:, lanes(c * 128, 128)], acts, sems(11),
    )
    query_sum = GradSum(
        me, lambda z, yh: h2.at[pl.ds(0, 256), lanes((z % 2) * 1024 + yh * 512 + (z // 2) * 256, 256)],
        lambda i: h2.at[pl.ds(256, 256), lanes(i * 256, 256)], o_q, 256,
        lambda v, c: v.at[:, lanes(c * 128, 128)], acts, sems(11),
    )
    gate_sum.start()
    up_sum.start()
    down_sum.start()
    base = sems(5)
    h1_over = send(h1, cfp, acts, base, partner)
    ot_over = send(ot.at[lanes((1 - core) * 256, 256)], hp.at[2, pl.ds(0, 256), pl.ds(0, 512)], acts, base + 1, partner)
    da_over = send(mf, h2p, acts, base + 2, partner)
    dq_over = send(qt.at[lanes((1 - core) * 256, 256)], hp.at[0, pl.ds(0, 256), pl.ds(0, 512)], acts, base + 3, partner)
    own_dkv = hp.at[1, pl.ds(256, 256), pl.ds(0, 512)]
    dkv_over = send(
        hp.at[1, lanes(256 + (1 - core) * 128, 128), pl.ds(0, 512)], hp.at[1, pl.ds(0, 128), pl.ds(0, 512)], acts, base + 4, partner
    )
    h1_over.start()
    ot_over.start()
    attend_back(0, 0, chunk_of[0] + 1)
    attend_back_end(0)
    ring_two[1].finish()
    da_over.start()
    d_attended(1)
    acc[...] = jnp.zeros(acc.shape, F32)

    def mixed_rows(h):
        rows = rows_of(h)
        total = x1[rows, :] + feed_sums[h].finish()
        squares[2:3, :] += column_squares(total)
        mix[rows, :] = total.astype(BF16)

    def homeward(src, home, at):
        def piece(q):
            half, block = q // 2, q % 2
            row = jnp.where(half == 0, me.quarter, 3 - me.quarter)
            return (
                src.at[lanes(half * 256, 256), lanes(block * 256, 256)],
                home.at[pl.ds(pl.multiple_of(row * CHUNK, CHUNK), CHUNK)],
            )

        copies = []
        for d in (1, 2, 3):
            s, t = piece((me.quarter + d) % 4)
            copies.append(send(s, t, acts, at + d, me.by_quarter(d)))
        s, t = piece(me.quarter)
        copies.append(pltpu.make_async_copy(s, t, acts[0].at[at]))
        return copies

    mixed_rows(0)
    mixed_rows(1)
    feed_sums[0].drain()
    feed_sums[1].drain()
    shake(1, [me.by_x(1), me.by_x(3)])
    home_mixed = homeward(mix, o_mixed, sems(4))
    for c in home_mixed:
        c.start()
    attend_back(1, 0, 3)
    gate_sum.sum_z()
    shake(2, ys_line)
    attend_back(1, 3, chunk_of[1] + 1)
    attend_back_end(1)
    dq_over.start()

    def dkv_slot(ref, k):
        return ref.at[k // 4, pl.ds(((k // 2) % 2) * 256, 256), pl.ds((k % 2) * 256, 256)]

    for j in range(8):
        dkv_slot(hid, j)[...] = dhf[:, j * CHUNK:(j + 1) * CHUNK].astype(BF16)
    base = sems(8)
    dkv_copies = []
    for d in (1, 2, 3):
        q = (me.quarter + d) % 4
        for h, k in ((0, q), (1, 7 - q)):
            src = hid.at[k // 4, lanes(((k // 2) % 2) * 256, 256), lanes((k % 2) * 256, 256)]
            dkv_copies.append(send(src, dkv_slot(dg, (d - 1) * 2 + h), acts, base + h * 4 + d, me.by_quarter(d)))
    for c in dkv_copies:
        c.start()
    da_over.wait()
    ot_over.wait()

    def out_grad(n, carry):
        cols = lanes(n * 256, 256)
        wo[lanes(core * 256, 256), cols] = (
            dot_plain(ot[lanes(core * 256, 256), :], mf[:, cols]) + dot_plain(hp[2, 0:256, 0:512], h2p[:, cols])
        ).astype(BF16)
        return carry

    lax.fori_loop(0, 8, out_grad, 0)
    shake(3, xs_line + ys_line + zs_line)
    unshake(2, ys_line)
    gate_sum.send_y()
    up_sum.sum_z()
    shake(4, ys_line)
    for c in dkv_copies:
        c.wait_recv()
    x1[...] = jnp.zeros(x1.shape, F32)
    for h in (0, 1):
        cols = slice(h * CHUNK, (h + 1) * CHUNK)
        total = dhf[:, lanes(chunk_of[h] * CHUNK, CHUNK)]
        for d in range(3):
            total = total + dkv_slot(dg, d * 2 + h)[...].astype(F32)
        for g in (0, 1):
            a, b = rope_rows(total[g * 64:g * 64 + 32], total[g * 64 + 32:g * 64 + 64], cosine[:, cols], -sine[:, cols])
            v = total[128 + g * 64:192 + g * 64]
            x1[pl.ds(heads[g], 32), cols] = a
            x1[pl.ds(heads[g] + 32, 32), cols] = b
            x1[pl.ds(256 + heads[g], 64), cols] = v
            hp[1, 256 + g * 64:288 + g * 64, cols] = a.astype(BF16)
            hp[1, 288 + g * 64:320 + g * 64, cols] = b.astype(BF16)
            hp[1, 384 + g * 64:448 + g * 64, cols] = v.astype(BF16)
    dkv_over.start()
    du[1, :, 0:512] = x1[...].T.astype(BF16)
    for c in dkv_copies:
        c.wait_send()
    unstash.wait()

    def back_one(h):
        rows = rows_of(h)

        def step(n, carry):
            feats = lanes(n * 256, 256)
            orig = lanes(((n % 2) * 4 + n // 2) * 256, 256)
            total = dot_nt(du[0, rows, 0:512], wq[feats, :])
            total = total + dot_nt(du[1, rows, 0:256], w_key[orig, :]) + dot_nt(du[1, rows, 256:512], w_value[orig, :])
            dhf[:, feats] = total
            return carry

        lax.fori_loop(0, 8, step, 0)
        norm_back(h, cf, r1, row_one, 0)

    row_one = device_order_row(gain1)
    unshake(1, [me.by_x(1), me.by_x(3)])
    one_sums = ring_sums()
    back_one(0)
    one_sums[0].start()
    back_one(1)
    one_sums[1].start()
    one_sums[0].turn()
    dkv_over.wait()
    dq_over.wait()
    h1_over.wait()

    def late_grads(n, carry):
        cols = lanes(n * 256, 256)
        mf[256:384, cols] = (
            dot_plain(hp[1, lanes(256 + core * 128, 128), 0:512], h1[:, cols]) + dot_plain(hp[1, 0:128, 0:512], cfp[:, cols])
        ).astype(BF16)
        h2[0:256, cols] = (
            dot_plain(qt[lanes(core * 256, 256), :], h1[:, cols]) + dot_plain(hp[0, 0:256, 0:512], cfp[:, cols])
        ).astype(BF16)
        return carry

    lax.fori_loop(0, 8, late_grads, 0)
    unshake(3, xs_line + ys_line + zs_line)
    base = sems(25)
    kv_z = [
        send(mf.at[pl.ds(256, 128), lanes(((me.z + d) % 4) * 512, 512)], mf.at[pl.ds(384, 128), pl.ds((d - 1) * 512, 512)],
             acts, base + d, me.by_z(d)) for d in (1, 2, 3)
    ]
    for c in kv_z:
        c.start()
    out_sum.start()
    query_sum.start()
    for k in range(2):
        small[k:k + 1, :] = gains[0:1, k * 1024:(k + 1) * 1024]
        small[2 + k:3 + k, :] = gains[1:2, k * 1024:(k + 1) * 1024]
    small[4:7, 0:512] = squares[0:3, :]

    def small_copies(n, peers, at):
        return [send(small, small_r.at[n, d], acts, at + d, p) for d, p in enumerate(peers)]

    def small_add(n, copies):
        for c in copies:
            c.wait()
        total = small[...]
        for d in range(len(copies)):
            total = total + small_r[n, d]
        small[...] = total

    small_z = small_copies(0, zs_line, sems(3))
    for c in small_z:
        c.start()
    one_sums[1].turn()
    unshake(4, ys_line)
    up_sum.send_y()
    down_sum.sum_z()
    shake(5, ys_line)

    def in_rows(h):
        rows = rows_of(h)
        dx1[rows, :] += one_sums[h].finish()

    in_rows(0)
    for c in kv_z:
        c.wait()
    z_at = lanes(me.z * 512, 512)
    mf[256:384, z_at] = (
        mf[256:384, z_at].astype(F32) + mf[384:512, 0:512].astype(F32) + mf[384:512, 512:1024].astype(F32)
        + mf[384:512, 1024:1536].astype(F32)
    ).astype(BF16)
    kv_y = [
        send(mf.at[pl.ds(256, 128), lanes(me.z * 512 + ((me.y + d) % 4) * 128, 128)],
             mf.at[pl.ds(384, 128), pl.ds(1536 + (d - 1) * 128, 128)], acts, base + 3 + d, me.by_y(d)) for d in (1, 2, 3)
    ]
    for c in kv_y:
        c.start()
    small_add(0, small_z)
    small_y = small_copies(1, ys_line, sems(3))
    for c in small_y:
        c.start()
    in_rows(1)
    home_in = homeward(dx1, o_in, sems(4))
    for c in home_in:
        c.start()
    unshake(5, ys_line)
    down_sum.send_y()
    out_sum.sum_z()
    query_sum.sum_z()
    shake(6, ys_line)
    for c in kv_y:
        c.wait()
    zy_at = lanes(me.z * 512 + me.y * 128, 128)
    mf[256:384, zy_at] = (
        mf[256:384, zy_at].astype(F32) + mf[384:512, 1536:1664].astype(F32) + mf[384:512, 1664:1792].astype(F32)
        + mf[384:512, 1792:1920].astype(F32)
    ).astype(BF16)
    pair = me.at(me.z, me.y, core, x + 1 - 2 * (x % 2))
    kv_pair = send(mf.at[pl.ds(256, 128), zy_at], mf.at[pl.ds(384, 128), pl.ds(1920, 128)], acts, base + 7, pair)
    kv_pair.start()
    small_add(1, small_y)
    small_x = small_copies(2, xs_line, sems(3))
    for c in small_x:
        c.start()
    unshake(6, ys_line)
    out_sum.send_y()
    query_sum.send_y()
    gate_sum.sum_y()
    up_sum.sum_y()
    kv_pair.wait()
    g_rows = lanes((x % 2) * 64, 64)
    mine = mf[pl.ds(pl.multiple_of(256 + (x % 2) * 64, 64), 64), zy_at].astype(F32)
    mine = mine + mf[pl.ds(pl.multiple_of(384 + (x % 2) * 64, 64), 64), 1920:2048].astype(F32)
    head_at = pl.ds(pl.multiple_of((2 * (x % 2) + x // 2) * 64, 64), 64)
    mf[head_at, zy_at] = mine.astype(BF16)
    kv_x = [send(mf.at[head_at, zy_at], mf.at[head_at, zy_at], acts, base + 7 + d, me.by_x(d)) for d in (1, 2, 3)]
    for c in kv_x:
        c.start()
    small_add(2, small_x)
    small_c = small_copies(3, [partner], sems(1))
    for c in small_c:
        c.start()
    for c in kv_x:
        c.wait()
    block = mf.at[pl.ds(0, 256), zy_at]
    kv_y2 = [send(block, block, acts, base + 11 + d, me.by_y(d)) for d in (1, 2, 3)]
    for c in kv_y2:
        c.start()
    down_sum.sum_y()
    small_add(3, small_c)
    for c in kv_y2:
        c.wait()
    block2 = mf.at[pl.ds(0, 256), z_at]
    kv_z2 = [send(block2, block2, acts, base + 15 + d, me.by_z(d)) for d in (1, 2, 3)]
    for c in kv_z2:
        c.start()
    out_sum.sum_y()
    query_sum.sum_y()
    small_out = pltpu.make_async_copy(small, o_small, lsem.at[8])
    small_out.start()
    for c in kv_z2:
        c.wait()
    kv_last = send(mf.at[pl.ds(0, 256)], o_kv.at[core], acts, base + 20, partner)
    kv_keep = pltpu.make_async_copy(mf.at[pl.ds(0, 256)], o_kv.at[core], lsem.at[9])
    kv_last.start()
    kv_keep.start()
    for s in (gate_sum, up_sum, down_sum, out_sum, query_sum):
        s.finish()
    for c in home_mixed + home_in:
        c.wait()
    for h in (0, 1):
        one_sums[h].drain()
    small_out.wait()
    kv_last.wait()
    kv_keep.wait()


ACTS = 220


def layer(tok, cot, wq, wo, wg, wu, wd, w_key, w_value, gain1, gain2, ids):
    ff = wg.shape[1]
    sds = jax.ShapeDtypeStruct
    outs = [
        sds((1024, 256), BF16), sds((1024, 256), F32), sds((256, 128), BF16), sds((256, 128), BF16),
        sds((128, ff), BF16), sds((128, ff), BF16), sds((ff, 128), BF16), sds((2, 256, 2048), BF16), sds((8, 1024), F32),
        sds((T, 2048), BF16),
    ]
    dma = pltpu.SemaphoreType.DMA
    vm = pl.BlockSpec(memory_space=pltpu.VMEM)
    wide = pltpu.VMEM((T, 2048), BF16)
    square = pltpu.VMEM((T, 512), BF16)
    inner = pltpu.VMEM((2, T, ff), BF16)
    row8 = pltpu.VMEM((8, CHUNK), F32)
    pair8 = pltpu.VMEM((2, 8, CHUNK), F32)
    return pl.pallas_call(
        layer_kernel, out_shape=outs, in_specs=[ANY] * 7 + [vm] * 5, out_specs=[ANY] * len(outs),
        scratch_shapes=[
            wide, wide, wide, wide, wide, wide,
            pltpu.VMEM((2048, 512), BF16), pltpu.VMEM((512, 2048), BF16),
            pltpu.VMEM((2, 2048, ff), BF16), pltpu.VMEM((2, 2048, ff), BF16), pltpu.VMEM((2, ff, 2048), BF16),
            square, square, square, pltpu.VMEM((8, 256, CHUNK), BF16),
            pltpu.VMEM((T, 512), F32), pltpu.VMEM((T, 512), F32),
            wide, pltpu.VMEM((2, 2, 256, 256), BF16), pltpu.VMEM((2, 2, 256, 512), BF16),
            pltpu.VMEM((512, CHUNK), F32), row8, row8, pair8, pair8,
            inner, inner, inner, pltpu.VMEM((3, T, ff), BF16), pltpu.VMEM((CHUNK, 2048), F32),
            pltpu.VMEM((T, 1), F32), pltpu.VMEM((T, 1), F32), square,
            pltpu.VMEM((2, 2048), F32), pltpu.VMEM((8, 512), F32), pltpu.VMEM((8, 1024), F32), pltpu.VMEM((4, 3, 8, 1024), F32),
            dma((ACTS,)), dma((ACTS,)), dma((5, 31)), dma((5, 31)), dma((10,)), pltpu.SemaphoreType.REGULAR((8,)),
        ],
        compiler_params=pltpu.CompilerParams(collective_id=0, has_side_effects=True, vmem_limit_bytes=64 << 20),
    )(tok, cot, wq, wo, wg, wu, wd, w_key, w_value, gain1, gain2, ids)


def from_device_order(v):
    return v.reshape((4, 2, 256) + v.shape[1:]).swapaxes(0, 1).reshape(v.shape)


def shards(tokens, segment_ids, norm_one, w_query, w_key, w_value, w_out, norm_two, w_gate, w_up, w_down, cotangent):
    mixed, input_grad, gq, go, gg, gu, gd, gkv, small, _ = layer(
        tokens, cotangent, w_query, w_out, w_gate, w_up, w_down, w_key, w_value,
        norm_one.reshape(1, 2048), norm_two.reshape(1, 2048), segment_ids.reshape(8, 16, 128),
    )
    key_total, value_total = [from_device_order(gkv[n].T.astype(F32)) for n in (0, 1)]
    rms = jnp.sqrt(jnp.sum(small[4:7, :512], 1) / (16384 * 2048))
    return (
        mixed, input_grad, gq.T.astype(F32), key_total, value_total, go.astype(F32), gg.astype(F32), gu.astype(F32),
        gd.astype(F32), from_device_order(small[0:2].reshape(2048)), from_device_order(small[2:4].reshape(2048)), rms,
    )


def solution(mesh):
    return jax.shard_map(
        shards,
        mesh=mesh,
        in_specs=(
            P("row", "col"), P(), P(), P("row", "col"), P(), P(), P("col", "row"), P(),
            P("row", "col"), P("row", "col"), P("col", "row"), P("row", "col"),
        ),
        out_specs=(
            P("row", "col"), P("row", "col"), P("row", "col"), P(), P(), P("col", "row"),
            P("row", "col"), P("row", "col"), P("col", "row"), P(), P(), P(),
        ),
        check_vma=False,
    )
```

time: 961 us -> 449 us (0.47)
  local copies, waits for them, and re-layouts: 204 us -> 27.6 us
  matrix products: 150 us -> 0 us
  other arithmetic: 86.3 us -> 6.29 us
  blocking collectives: 65.5 us -> 0 us
  Pallas kernels: 428 us -> 407 us
  between operations: 16 us -> 1.13 us
    dot_general x64 -> x0, matrix products: 150 us -> none  [the longest x25 69.8 us: dot_nt(): lax.dot_general(left, right, (((1,), (1,)), ((), ())), preferred_element_...]
    reshape x26 -> x5, local copies, waits for them, and re-layouts: 85.2 us -> 16.4 us  [the longest x4 15.1 us: from_device_order(): return v.reshape((4, 2, 256) + v.shape[1:]).swapaxes(0, 1).reshape(v.shape)]
    psum x1 -> x0, blocking collectives: 65.5 us -> none  [shards(): lax.psum((gain_one_grad, gain_two_grad, stats), ('row', 'col'))]
    transpose x13 -> x0, local copies, waits for them, and re-layouts: 54.3 us -> none  [the longest x4 35 us: by_row(): return v.transpose(3, 2, 0, 1, 4, 5).reshape(2, 4, 2, 128, cols)]
    convert_element_type x26 -> x3, other arithmetic: 40.6 us -> 1.44 us  [the longest x1 0.76 us: shards(): gd.astype(F32)]
    unnamed x169 -> x23, local copies, waits for them, and re-layouts: 43.9 us -> 8.97 us
    reduce_sum x19 -> x1, other arithmetic: 23.8 us -> 0.96 us  [shards(): rms = jnp.sqrt(jnp.sum(small[4:7, :512], 1) / (16384 * 2048))]
    pallas_call x11 -> x1, Pallas kernels: 428 us -> 407 us  [layer(): pl.pallas_call(layer_kernel, out_shape=outs, in_specs=[ANY] * 7 + [vm] *...]
  transfers between devices with their start and end apart: 1 -> 0, of which waited for: 0 -> 0; matrix products, arithmetic and copies ran while one was open for 8% -> 0% of each run, Pallas kernels for 8% -> 0%
where the time goes in v1:
time: 449 us; the launch traced here: 442 us
  Pallas kernels  407 us (91%)
  local copies, waits for them, and re-layouts  27.6 us (6%)
  other arithmetic  6.29 us (1%)
    pallas_call x1, Pallas kernels, layer(): pl.pallas_call(layer_kernel, out_shape=outs, in_specs=[ANY] * 7 + [vm] *...  407 us
    reshape x4, local copies, waits for them, and re-layouts, from_device_order(): return v.reshape((4, 2, 256) + v.shape[1:]).swapaxes(0, 1).reshape(v.shape)  15.1 us

profile of v1, /device:TPU:1, one launch (start us, length us, event | category | flops | bytes accessed | tf_op | source)
XLA Modules:
  0.0 442.4 jit_solution(17687258744008255258)
XLA Ops:
  0.6 1.7 copy.31.wg_s
  2.4 1.7 copy.32.wu_s
  4.1 1.3 reshape.63.gain1
  5.4 1.3 reshape.64.gain2
  6.7 407.4 %shard_map.211 = (bf16[1024,256]{1,0:T(8,128)(2,1)}, f32[1024,256]{1,0:T(8,128)}, bf16[256,128]{1,0:T(8,128)(2,1)}, bf16[256,128]{1,0:T(8,128)(2,1)}, bf16[128,7...) custom-call(bf16[1024,256]{1,0:T(8,128)(2,1)} %tok.1, ...), custom_call_target="tpu_custom_call" | custom-call | tf_op jit(solution)/shard_map/pallas_call | solution.py:1118
  414.1 0.8 fusion
  414.9 0.6 copy.40
  415.6 0.6 copy.41
  416.2 3.4 convert_bitcast_fusion
  419.6 4.0 reshape.81
  423.6 4.1 copy.33
  427.7 2.8 reshape.83
  430.5 0.0 copy-start.4
  430.5 0.0 copy-start.3
  430.5 0.0 copy-start.2
  430.5 4.2 copy.34
  434.7 1.0 slice_reduce_fusion
  435.7 0.5 multiply_sqrt_fusion
  436.2 0.0 copy-done.4
  436.2 0.8 convert_element_type.41
  437.0 0.0 copy-done.3
  437.0 0.9 copy.38
  437.8 0.0 copy-done.2
  437.8 0.9 copy.39
  438.7 0.0 copy-done.6
  438.7 0.8 copy.37
  439.5 0.0 copy-done.5
  439.5 0.7 convert_element_type.38
  440.2 0.0 copy-done.1
  440.2 0.8 copy.48
  441.0 0.0 copy-done
  441.0 1.0 copy.49
  (9 shorter events, 0.1 us)
Async XLA Ops:
  430.5 5.7 %copy-start.4 = (bf16[704,128]{1,0:T(8,128)(2,1)S(1)}, bf16[704,128]{1,0:T(8,128)(2,1)}, u32[]{:S(2)}) copy-start(bf16[704,128]{1,0:T(8,128)(2,1)} %get-tuple-element.28) | copy-start | bytes 540676
  430.5 6.4 %copy-start.3 = (bf16[128,704]{1,0:T(8,128)(2,1)S(1)}, bf16[128,704]{1,0:T(8,128)(2,1)}, u32[]{:S(2)}) copy-start(bf16[128,704]{1,0:T(8,128)(2,1)} %get-tuple-element.26) | copy-start | bytes 540676
  430.5 7.3 %copy-start.2 = (bf16[128,704]{1,0:T(8,128)(2,1)S(1)}, bf16[128,704]{1,0:T(8,128)(2,1)}, u32[]{:S(2)}) copy-start(bf16[128,704]{1,0:T(8,128)(2,1)} %get-tuple-element.27) | copy-start | bytes 540676
  430.5 8.2 %copy-start.6 = (bf16[256,128]{1,0:T(8,128)(2,1)S(1)}, bf16[256,128]{1,0:T(8,128)(2,1)}, u32[]{:S(2)}) copy-start(bf16[256,128]{1,0:T(8,128)(2,1)} %get-tuple-element.23) | copy-start | bytes 196612
  434.7 4.8 %copy-start.5 = (bf16[256,128]{1,0:T(8,128)(2,1)S(1)}, bf16[256,128]{1,0:T(8,128)(2,1)}, u32[]{:S(2)}) copy-start(bf16[256,128]{1,0:T(8,128)(2,1)} %get-tuple-element.25) | copy-start | bytes 196612
  434.7 5.4 %copy-start.1 = (bf16[1024,256]{1,0:T(8,128)(2,1)S(1)}, bf16[1024,256]{1,0:T(8,128)(2,1)}, u32[]{:S(2)}) copy-start(bf16[1024,256]{1,0:T(8,128)(2,1)} %get-tuple-element.70) | copy-start | bytes 1572868
  434.7 6.2 %copy-start = (f32[1024,256]{1,0:T(8,128)S(1)}, f32[1024,256]{1,0:T(8,128)}, u32[]{:S(2)}) copy-start(f32[1024,256]{1,0:T(8,128)} %get-tuple-element.71) | copy-start | bytes 3145732

commit v2 on v1

--- a/solution.py
+++ b/solution.py
@@ -139,13 +139,16 @@
 
         each(3, arrived)
 
-    def cross(self):
+    def cross(self, k=None):
         def arrived(j):
-            k, i = j // 3, j % 3
-            self.second(k, i).wait_recv()
-            self.third(k * 4 + i + 1).start()
-
-        each(12, arrived)
+            n, i = j // 3, j % 3
+            self.second(n, i).wait_recv()
+            self.third(n * 4 + i + 1).start()
+
+        if k is None:
+            each(12, arrived)
+        else:
+            each(3, lambda i: arrived(k * 3 + i))
 
     def finish(self):
         each(16, lambda i: self.third(i).wait_recv())
@@ -383,6 +386,92 @@
         for yh in (0, 1):
             step, copy = self.second(yh)
             pl.when(step != 0)(copy.wait_send)
+
+
+class GradSumY(GradSum):
+    def __init__(self, me, own, land, extra, out, rows, halves, sems, base):
+        super().__init__(me, own, land, out, rows, halves, sems, base)
+        self.extra = extra
+
+    def landing(self, step, k):
+        return self.extra(k) if step == 3 else self.land((step - 1) * 4 + k)
+
+    def first_y(self, yh, step, k):
+        me = self.me
+        return pltpu.make_async_remote_copy(
+            src_ref=self.own(k, yh), dst_ref=self.landing(step, k), send_sem=self.sems[0].at[self.base + yh * 4 + k],
+            recv_sem=self.sems[1].at[self.base + (step - 1) * 4 + k],
+            device_id=me.at(me.z, yh * 2 + me.core, me.core, me.x), device_id_type=MESH,
+        )
+
+    def steps(self, act):
+        me = self.me
+        for yh in (0, 1):
+            away = (yh * 2 + me.core + 4 - me.y) % 4
+            for step in (1, 2, 3):
+                pl.when(away == step)(functools.partial(act, yh, step))
+
+    def start(self):
+        self.steps(lambda yh, step: each(4, lambda k: self.first_y(yh, step, k).start()))
+
+    def sum_y(self):
+        me = self.me
+
+        def work():
+            for step in (1, 2, 3):
+                each(4, lambda k: self.first_y(0, step, k).wait_recv())
+
+            def one(k):
+                self.add(self.own(k, me.yh), [self.landing(step, k) for step in (1, 2, 3)])
+
+            each(4, one)
+
+        pl.when(me.yl == me.core)(work)
+        self.steps(lambda yh, step: each(4, lambda k: self.first_y(yh, step, k).wait_send()))
+
+    def second_z(self, d):
+        me = self.me
+        return send(self.own((me.z + d) % 4, me.yh), self.land(d - 1), self.sems, self.base + 11 + d, me.by_z(d))
+
+    def send_z(self):
+        def work():
+            for d in (1, 2, 3):
+                self.second_z(d).start()
+
+        pl.when(self.me.yl == self.me.core)(work)
+
+    def last(self):
+        me = self.me
+        view = self.halves(self.own(me.z, me.yh), 1 - me.core)
+        return send(view, self.out, self.sems, self.base + 15, me.partner())
+
+    def keep(self):
+        me = self.me
+        return pltpu.make_async_copy(self.halves(self.own(me.z, me.yh), me.core), self.out, self.sems[0].at[self.base + 16])
+
+    def sum_z(self):
+        me = self.me
+
+        def work():
+            for d in (1, 2, 3):
+                self.second_z(d).wait_recv()
+            self.add(self.own(me.z, me.yh), [self.land(d) for d in range(3)])
+            self.last().start()
+            self.keep().start()
+
+        pl.when(me.yl == me.core)(work)
+
+    def finish(self):
+        me = self.me
+
+        def sender():
+            for d in (1, 2, 3):
+                self.second_z(d).wait_send()
+            self.last().wait_send()
+            self.keep().wait()
+
+        pl.when(me.yl == me.core)(sender)
+        pl.when(me.yl != me.core)(lambda: self.last().wait_recv())
 
 
 def layer_kernel(
@@ -417,7 +506,7 @@
     partner = me.partner()
     greet(xs_line + ys_line + zs_line + four)
     slots = weight_slots(wq, wo, wg, wu, wd)
-    first_z = (True, True, True, False, False)
+    first_z = (False, True, False, True, False)
     spreads = [
         Spread(me, src, slots[n], first_z[n], (w_s.at[n], w_r.at[n]), lsem.at[2 + n])
         for n, src in enumerate((wq_s, wo_s, wg_s, wu_s, wd_s))
@@ -426,10 +515,8 @@
     cot_copies, cot_local = reshard_in(me, cot, cf, acts, sems(4), lsem.at[1])
     for c in in_copies + [in_local]:
         c.start()
-    for s in spreads:
-        s.start()
-    for c in cot_copies + [cot_local]:
-        c.start()
+    s_q, s_o, s_g, s_u, s_d = spreads
+    s_q.start()
     seq = me.z * 2 + me.yh
     chunk_of = (me.quarter, 7 - me.quarter)
     lane = lax.broadcasted_iota(jnp.int32, (1, CHUNK), 1)
@@ -448,25 +535,30 @@
     in_local.wait()
     ring_tok = Ring(me, xf, pl.ds(0, T), acts, sems(4))
     ring_tok.start()
-    spreads[0].turn()
-    spreads[1].turn()
+    s_q.turn()
+    s_g.start()
+    for c in cot_copies + [cot_local]:
+        c.start()
+    s_d.start()
+    s_o.start()
+    s_u.start()
+    ring_tok.turn()
+    ring_cot = Ring(me, cf, pl.ds(0, T), acts, sems(4))
+    s_q.cross()
+    ring_tok.finish()
+    s_g.turn()
+    s_d.turn()
     for c in cot_copies:
         c.wait_recv()
     cot_local.wait()
-    ring_tok.turn()
-    ring_cot = Ring(me, cf, pl.ds(0, T), acts, sems(4))
     ring_cot.start()
-    spreads[0].cross()
-    for s in spreads[2:]:
-        s.turn()
-    ring_tok.finish()
     for c in in_copies + cot_copies:
         c.wait_send()
     stash = pltpu.make_async_copy(xf, xs, lsem.at[7])
     stash.start()
 
     rms_rows(xf, device_order_row(gain1), h1, r1, 0, T)
-    spreads[0].finish()
+    s_q.finish()
     for n, w in enumerate((w_key, w_value)):
         total = None
         for p, b in enumerate(ORIGINAL):
@@ -499,9 +591,9 @@
             qt[n * 256 + at:n * 256 + at + 32, :] = (a * 0.125).astype(BF16)
             qt[n * 256 + at + 32:n * 256 + at + 64, :] = (b * 0.125).astype(BF16)
     ring_cot.turn()
-    spreads[1].cross()
     for c in kv_copies:
         c.wait()
+    s_o.turn()
 
     def row_form(block):
         return block.astype(F32).T.astype(BF16)
@@ -580,14 +672,14 @@
     attend_begin()
     attend(0, 0, chunk_of[0] + 1)
     attend_end(0)
-    spreads[1].finish()
+    s_u.turn()
+    s_o.cross()
+    s_o.finish()
     project(0)
     sums[0].start()
     attend_begin()
     attend(1, 0, 3)
     sums[0].turn()
-    for s in spreads[2:]:
-        s.cross()
     attend(1, 3, chunk_of[1] + 1)
     attend_end(1)
     stream(0)
@@ -607,8 +699,10 @@
     row_two = device_order_row(gain2)
     rms_rows(mf, row_two, h2, r2, 0, CHUNK)
     for s in spreads[2:]:
+        s.cross()
+    ring[1].turn()
+    for s in spreads[2:]:
         s.finish()
-    ring[1].turn()
 
     def feed_forward(h):
         rows = rows_of(h)
@@ -712,19 +806,17 @@
     grads_in(0, 4)
     back_two_sums[1].turn()
     ring_two[0].turn()
-    back_two_sums[0].drain()
-    feed_sums = ring_sums()
-    feed(0)
-    feed_sums[0].start()
     grads_in(4, 8)
     d_stream(1)
     ring_two[1].start()
     ring_two[0].finish()
-    back_two_sums[1].drain()
+    for h in (0, 1):
+        back_two_sums[h].drain()
+    feed_sums = ring_sums()
+    feed(0)
+    feed(1)
     ring_two[1].turn()
-    feed(1)
-    feed_sums[1].start()
-    feed_sums[0].turn()
+    feed_sums[0].start()
 
     for at, size in ((0, 256), (256, 256), (512, 192)):
         mine = hid[core, :, at:at + size].T
@@ -792,15 +884,21 @@
     d_attended(0)
     dhf[...] = jnp.zeros(dhf.shape, F32)
     acc[...] = jnp.zeros(acc.shape, F32)
-    feed_sums[1].turn()
     unshake(0, zs_line + ys_line + four)
     ff = wg.shape[2]
-    gate_sum, up_sum = [
-        GradSum(
-            me, lambda z, yh, w=w: w.at[core, lanes((z % 2) * 1024 + yh * 512 + (z // 2) * 256, 256)],
-            lambda i, w=w: w.at[1 - core, lanes(i * 256, 256)], out, 256, lambda v, c: v.at[lanes(c * 128, 128)], acts, sems(11),
-        ) for w, out in ((wg, o_gate), (wu, o_up))
-    ]
+    def row_slot(w):
+        return lambda z, yh: w.at[core, lanes((z % 2) * 1024 + yh * 512 + (z // 2) * 256, 256)]
+
+    def row_land(w):
+        return lambda i: w.at[1 - core, lanes(i * 256, 256)]
+
+    def row_half(v, c):
+        return v.at[lanes(c * 128, 128)]
+
+    gate_sum = GradSum(me, row_slot(wg), row_land(wg), o_gate, 256, row_half, acts, sems(11))
+    up_sum = GradSumY(
+        me, row_slot(wu), row_land(wu), lambda k: hp.at[k // 2, lanes((k % 2) * 256, 256)], o_up, 256, row_half, acts, sems(17)
+    )
     down_sum = GradSum(
         me, lambda z, yh: wd.at[core, :, lanes((z % 2) * 1024 + yh * 512 + (z // 2) * 256, 256)],
         lambda i: wd.at[1 - core, :, lanes(i * 256, 256)], o_down, ff, lambda v, c: v.at[:, lanes(c * 128, 128)], acts, sems(11),
@@ -815,23 +913,22 @@
         lambda i: h2.at[pl.ds(256, 256), lanes(i * 256, 256)], o_q, 256,
         lambda v, c: v.at[:, lanes(c * 128, 128)], acts, sems(11),
     )
+    up_sum.start()
     gate_sum.start()
-    up_sum.start()
     down_sum.start()
     base = sems(5)
     h1_over = send(h1, cfp, acts, base, partner)
     ot_over = send(ot.at[lanes((1 - core) * 256, 256)], hp.at[2, pl.ds(0, 256), pl.ds(0, 512)], acts, base + 1, partner)
     da_over = send(mf, h2p, acts, base + 2, partner)
-    dq_over = send(qt.at[lanes((1 - core) * 256, 256)], hp.at[0, pl.ds(0, 256), pl.ds(0, 512)], acts, base + 3, partner)
-    own_dkv = hp.at[1, pl.ds(256, 256), pl.ds(0, 512)]
-    dkv_over = send(
-        hp.at[1, lanes(256 + (1 - core) * 128, 128), pl.ds(0, 512)], hp.at[1, pl.ds(0, 128), pl.ds(0, 512)], acts, base + 4, partner
-    )
+    dq_over = send(qt.at[lanes((1 - core) * 256, 256)], hp.at[2, pl.ds(256, 256), pl.ds(0, 512)], acts, base + 3, partner)
+    dkv_over = send(dg.at[1, lanes(256 + (1 - core) * 128, 128), pl.ds(0, 512)], o_r.at[pl.ds(0, 128)], acts, base + 4, partner)
     h1_over.start()
     ot_over.start()
     attend_back(0, 0, chunk_of[0] + 1)
     attend_back_end(0)
     ring_two[1].finish()
+    feed_sums[1].start()
+    feed_sums[0].turn()
     da_over.start()
     d_attended(1)
     acc[...] = jnp.zeros(acc.shape, F32)
@@ -859,17 +956,8 @@
         copies.append(pltpu.make_async_copy(s, t, acts[0].at[at]))
         return copies
 
-    mixed_rows(0)
-    mixed_rows(1)
-    feed_sums[0].drain()
-    feed_sums[1].drain()
-    shake(1, [me.by_x(1), me.by_x(3)])
-    home_mixed = homeward(mix, o_mixed, sems(4))
-    for c in home_mixed:
-        c.start()
     attend_back(1, 0, 3)
-    gate_sum.sum_z()
-    shake(2, ys_line)
+    feed_sums[1].turn()
     attend_back(1, 3, chunk_of[1] + 1)
     attend_back_end(1)
     dq_over.start()
@@ -888,6 +976,14 @@
             dkv_copies.append(send(src, dkv_slot(dg, (d - 1) * 2 + h), acts, base + h * 4 + d, me.by_quarter(d)))
     for c in dkv_copies:
         c.start()
+    mixed_rows(0)
+    mixed_rows(1)
+    feed_sums[0].drain()
+    feed_sums[1].drain()
+    shake(1, [me.by_x(1), me.by_x(3)])
+    home_mixed = homeward(mix, o_mixed, sems(4))
+    for c in home_mixed:
+        c.start()
     da_over.wait()
     ot_over.wait()
 
@@ -900,10 +996,8 @@
 
     lax.fori_loop(0, 8, out_grad, 0)
     shake(3, xs_line + ys_line + zs_line)
-    unshake(2, ys_line)
-    gate_sum.send_y()
-    up_sum.sum_z()
-    shake(4, ys_line)
+    up_sum.sum_y()
+    shake(4, zs_line)
     for c in dkv_copies:
         c.wait_recv()
     x1[...] = jnp.zeros(x1.shape, F32)
@@ -918,9 +1012,9 @@
             x1[pl.ds(heads[g], 32), cols] = a
             x1[pl.ds(heads[g] + 32, 32), cols] = b
             x1[pl.ds(256 + heads[g], 64), cols] = v
-            hp[1, 256 + g * 64:288 + g * 64, cols] = a.astype(BF16)
-            hp[1, 288 + g * 64:320 + g * 64, cols] = b.astype(BF16)
-            hp[1, 384 + g * 64:448 + g * 64, cols] = v.astype(BF16)
+            dg[1, 256 + g * 64:288 + g * 64, cols] = a.astype(BF16)
+            dg[1, 288 + g * 64:320 + g * 64, cols] = b.astype(BF16)
+            dg[1, 384 + g * 64:448 + g * 64, cols] = v.astype(BF16)
     dkv_over.start()
     du[1, :, 0:512] = x1[...].T.astype(BF16)
     for c in dkv_copies:
@@ -956,10 +1050,10 @@
     def late_grads(n, carry):
         cols = lanes(n * 256, 256)
         mf[256:384, cols] = (
-            dot_plain(hp[1, lanes(256 + core * 128, 128), 0:512], h1[:, cols]) + dot_plain(hp[1, 0:128, 0:512], cfp[:, cols])
+            dot_plain(dg[1, lanes(256 + core * 128, 128), 0:512], h1[:, cols]) + dot_plain(o_r[0:128, :], cfp[:, cols])
         ).astype(BF16)
         h2[0:256, cols] = (
-            dot_plain(qt[lanes(core * 256, 256), :], h1[:, cols]) + dot_plain(hp[0, 0:256, 0:512], cfp[:, cols])
+            dot_plain(qt[lanes(core * 256, 256), :], h1[:, cols]) + dot_plain(hp[2, 256:512, 0:512], cfp[:, cols])
         ).astype(BF16)
         return carry
 
@@ -994,8 +1088,10 @@
     for c in small_z:
         c.start()
     one_sums[1].turn()
-    unshake(4, ys_line)
-    up_sum.send_y()
+    unshake(4, zs_line)
+    up_sum.send_z()
+    gate_sum.sum_z()
+    shake(2, ys_line)
     down_sum.sum_z()
     shake(5, ys_line)
 
@@ -1025,6 +1121,8 @@
     home_in = homeward(dx1, o_in, sems(4))
     for c in home_in:
         c.start()
+    unshake(2, ys_line)
+    gate_sum.send_y()
     unshake(5, ys_line)
     down_sum.send_y()
     out_sum.sum_z()
@@ -1048,7 +1146,7 @@
     out_sum.send_y()
     query_sum.send_y()
     gate_sum.sum_y()
-    up_sum.sum_y()
+    up_sum.sum_z()
     kv_pair.wait()
     g_rows = lanes((x % 2) * 64, 64)
     mine = mf[pl.ds(pl.multiple_of(256 + (x % 2) * 64, 64), 64), zy_at].astype(F32)
@@ -1082,10 +1180,28 @@
     small_out.start()
     for c in kv_z2:
         c.wait()
-    kv_last = send(mf.at[pl.ds(0, 256)], o_kv.at[core], acts, base + 20, partner)
-    kv_keep = pltpu.make_async_copy(mf.at[pl.ds(0, 256)], o_kv.at[core], lsem.at[9])
+    kv_last = send(mf.at[pl.ds(0, 256)], mf.at[pl.ds(256, 256)], acts, base + 20, partner)
     kv_last.start()
-    kv_keep.start()
+    flights = []
+
+    def lay_out(home, first, k):
+        for p, b in enumerate(ORIGINAL):
+            spot = (k * 8 + p) % 4
+            if len(flights) >= 4:
+                flights[-4].wait()
+            stage = x1.at[pl.ds((spot // 2) * 256, 256), pl.ds((spot % 2) * 256, 256)]
+            x1[(spot // 2) * 256:(spot // 2 + 1) * 256, (spot % 2) * 256:(spot % 2 + 1) * 256] = (
+                mf[first:first + 256, p * 256:(p + 1) * 256].astype(F32).T
+            )
+            copy = pltpu.make_async_copy(stage, home.at[pl.ds(b * 256, 256)], lsem.at[10 + spot])
+            copy.start()
+            flights.append(copy)
+
+    lay_out(o_kv.at[core], 0, 0)
+    kv_last.wait()
+    lay_out(o_kv.at[1 - core], 256, 1)
+    for c in flights[-4:]:
+        c.wait()
     for s in (gate_sum, up_sum, down_sum, out_sum, query_sum):
         s.finish()
     for c in home_mixed + home_in:
@@ -1093,11 +1209,9 @@
     for h in (0, 1):
         one_sums[h].drain()
     small_out.wait()
-    kv_last.wait()
-    kv_keep.wait()
-
-
-ACTS = 220
+
+
+ACTS = 240
 
 
 def layer(tok, cot, wq, wo, wg, wu, wd, w_key, w_value, gain1, gain2, ids):
@@ -1105,7 +1219,7 @@
     sds = jax.ShapeDtypeStruct
     outs = [
         sds((1024, 256), BF16), sds((1024, 256), F32), sds((256, 128), BF16), sds((256, 128), BF16),
-        sds((128, ff), BF16), sds((128, ff), BF16), sds((ff, 128), BF16), sds((2, 256, 2048), BF16), sds((8, 1024), F32),
+        sds((128, ff), BF16), sds((128, ff), BF16), sds((ff, 128), BF16), sds((2, 2048, 256), F32), sds((8, 1024), F32),
         sds((T, 2048), BF16),
     ]
     dma = pltpu.SemaphoreType.DMA
@@ -1128,7 +1242,7 @@
             inner, inner, inner, pltpu.VMEM((3, T, ff), BF16), pltpu.VMEM((CHUNK, 2048), F32),
             pltpu.VMEM((T, 1), F32), pltpu.VMEM((T, 1), F32), square,
             pltpu.VMEM((2, 2048), F32), pltpu.VMEM((8, 512), F32), pltpu.VMEM((8, 1024), F32), pltpu.VMEM((4, 3, 8, 1024), F32),
-            dma((ACTS,)), dma((ACTS,)), dma((5, 31)), dma((5, 31)), dma((10,)), pltpu.SemaphoreType.REGULAR((8,)),
+            dma((ACTS,)), dma((ACTS,)), dma((5, 31)), dma((5, 31)), dma((14,)), pltpu.SemaphoreType.REGULAR((8,)),
         ],
         compiler_params=pltpu.CompilerParams(collective_id=0, has_side_effects=True, vmem_limit_bytes=64 << 20),
     )(tok, cot, wq, wo, wg, wu, wd, w_key, w_value, gain1, gain2, ids)
@@ -1143,7 +1257,7 @@
         tokens, cotangent, w_query, w_out, w_gate, w_up, w_down, w_key, w_value,
         norm_one.reshape(1, 2048), norm_two.reshape(1, 2048), segment_ids.reshape(8, 16, 128),
     )
-    key_total, value_total = [from_device_order(gkv[n].T.astype(F32)) for n in (0, 1)]
+    key_total, value_total = gkv[0], gkv[1]
     rms = jnp.sqrt(jnp.sum(small[4:7, :512], 1) / (16384 * 2048))
     return (
         mixed, input_grad, gq.T.astype(F32), key_total, value_total, go.astype(F32), gg.astype(F32), gu.astype(F32),

time: 449 us -> 366 us (0.82); the launches traced: 442 us -> 366 us
  Pallas kernels: 407 us -> 345 us
  local copies, waits for them, and re-layouts: 27.6 us -> 17 us
    pallas_call x1, Pallas kernels: 407 us -> 345 us  [layer(): pl.pallas_call(layer_kernel, out_shape=outs, in_specs=[ANY] * 7 + [vm] *...]
    reshape x4 -> x0, local copies, waits for them, and re-layouts: 15.1 us -> none  [from_device_order(): return v.reshape((4, 2, 256) + v.shape[1:]).swapaxes(0, 1).reshape(v.shape)]
    squeeze x0 -> x1, local copies, waits for them, and re-layouts: none -> 4.57 us  [shards(): key_total, value_total = (gkv[0], gkv[1])]
where the time goes in v2:
time: 366 us
  Pallas kernels  345 us (94%)
  local copies, waits for them, and re-layouts  17 us (5%)
    pallas_call x1, Pallas kernels, layer(): pl.pallas_call(layer_kernel, out_shape=outs, in_specs=[ANY] * 7 + [vm] *...  345 us
    unnamed x23, local copies, waits for them, and re-layouts  8.97 us

profile of v2, /device:TPU:1, one launch (start us, length us, event | category | flops | bytes accessed | tf_op | source)
XLA Modules:
  0.0 365.8 jit_solution(13641406663139035927)
XLA Ops:
  0.6 1.7 copy.29.wg_s
  2.4 1.7 copy.30.wu_s
  4.1 1.3 reshape.39.gain1
  5.4 1.3 reshape.40.gain2
  6.7 345.2 %shard_map.211 = (bf16[1024,256]{1,0:T(8,128)(2,1)}, f32[1024,256]{1,0:T(8,128)}, bf16[256,128]{1,0:T(8,128)(2,1)}, bf16[256,128]{1,0:T(8,128)(2,1)}, bf16[128,7...) custom-call(bf16[1024,256]{1,0:T(8,128)(2,1)} %tok.1, ...), custom_call_target="tpu_custom_call" | custom-call | tf_op jit(solution)/shard_map/pallas_call | solution.py:1232
  351.9 0.8 fusion
  352.8 0.6 copy.36
  353.4 0.6 copy.37
  354.0 0.0 copy-start.4
  354.0 0.0 copy-start.3
  354.0 0.0 copy-start.2
  354.0 0.0 copy-start.6
  354.0 4.6 %slice_bitcast_fusion = (f32[2048,256]{1,0:T(8,128)}, f32[2048,256]{1,0:T(8,128)}) fusion(f32[2,2048,256]{2,1,0:T(8,128)} %get-tuple-element.24), kind=kLoop, calls=%fused_computation | loop fusion | bytes 8388608 | tf_op jit(solution)/shard_map/squeeze | solution.py:1260
  358.6 0.0 copy-start.5
  358.6 0.0 copy-start.1
  358.6 0.0 copy-start
  358.6 1.0 slice_reduce_fusion
  359.5 0.5 multiply_sqrt_fusion
  360.1 0.0 copy-done.4
  360.1 0.8 convert_element_type.23
  360.8 0.0 copy-done.3
  360.8 0.9 copy.34
  361.7 0.0 copy-done.2
  361.7 0.9 copy.35
  362.6 0.0 copy-done.6
  362.6 0.8 copy.33
  363.4 0.0 copy-done.5
  363.4 0.7 convert_element_type.20
  364.0 0.0 copy-done.1
  364.0 0.8 copy.44
  364.8 0.0 copy-done
  364.8 1.0 copy.45
  (5 shorter events, 0.1 us)
Async XLA Ops:
  354.0 6.1 %copy-start.4 = (bf16[704,128]{1,0:T(8,128)(2,1)S(1)}, bf16[704,128]{1,0:T(8,128)(2,1)}, u32[]{:S(2)}) copy-start(bf16[704,128]{1,0:T(8,128)(2,1)} %get-tuple-element.28) | copy-start | bytes 540676
  354.0 6.8 %copy-start.3 = (bf16[128,704]{1,0:T(8,128)(2,1)S(1)}, bf16[128,704]{1,0:T(8,128)(2,1)}, u32[]{:S(2)}) copy-start(bf16[128,704]{1,0:T(8,128)(2,1)} %get-tuple-element.26) | copy-start | bytes 540676
  354.0 7.7 %copy-start.2 = (bf16[128,704]{1,0:T(8,128)(2,1)S(1)}, bf16[128,704]{1,0:T(8,128)(2,1)}, u32[]{:S(2)}) copy-start(bf16[128,704]{1,0:T(8,128)(2,1)} %get-tuple-element.27) | copy-start | bytes 540676
  354.0 8.6 %copy-start.6 = (bf16[256,128]{1,0:T(8,128)(2,1)S(1)}, bf16[256,128]{1,0:T(8,128)(2,1)}, u32[]{:S(2)}) copy-start(bf16[256,128]{1,0:T(8,128)(2,1)} %get-tuple-element.23) | copy-start | bytes 196612
  358.6 4.8 %copy-start.5 = (bf16[256,128]{1,0:T(8,128)(2,1)S(1)}, bf16[256,128]{1,0:T(8,128)(2,1)}, u32[]{:S(2)}) copy-start(bf16[256,128]{1,0:T(8,128)(2,1)} %get-tuple-element.25) | copy-start | bytes 196612
  358.6 5.4 %copy-start.1 = (bf16[1024,256]{1,0:T(8,128)(2,1)S(1)}, bf16[1024,256]{1,0:T(8,128)(2,1)}, u32[]{:S(2)}) copy-start(bf16[1024,256]{1,0:T(8,128)(2,1)} %get-tuple-element.70) | copy-start | bytes 1572868
  358.6 6.2 %copy-start = (f32[1024,256]{1,0:T(8,128)S(1)}, f32[1024,256]{1,0:T(8,128)}, u32[]{:S(2)}) copy-start(f32[1024,256]{1,0:T(8,128)} %get-tuple-element.71) | copy-start | bytes 3145732

commit v3 on v2

--- a/solution.py
+++ b/solution.py
@@ -580,9 +580,10 @@
     for h in (0, 1):
         for d in (1, 2, 3):
             block = kvt.at[chunk_of[h]]
-            kv_copies.append(send(block, block, acts, base + h * 4 + d, me.by_quarter(d)))
-    for c in kv_copies:
-        c.start()
+            copy = send(block, block, acts, base + h * 4 + d, me.by_quarter(d))
+            kv_copies.append((copy, h == 0 or (me.quarter + d) % 4 <= me.quarter, h == 0 or me.quarter <= (me.quarter + 4 - d) % 4))
+    for c, goes, _ in kv_copies:
+        pl.when(goes)(c.start)
     for n in (0, 1):
         q = dot_plain(h1[...], wq[:, n * 256:(n + 1) * 256]).T
         for hd in range(4):
@@ -591,8 +592,9 @@
             qt[n * 256 + at:n * 256 + at + 32, :] = (a * 0.125).astype(BF16)
             qt[n * 256 + at + 32:n * 256 + at + 64, :] = (b * 0.125).astype(BF16)
     ring_cot.turn()
-    for c in kv_copies:
-        c.wait()
+    for c, goes, comes in kv_copies:
+        pl.when(comes)(c.wait_recv)
+        pl.when(goes)(c.wait_send)
     s_o.turn()
 
     def row_form(block):
@@ -777,6 +779,35 @@
 
     d_stream(0)
     ring_two[0].start()
+    ff = wg.shape[2]
+
+    def row_slot(w):
+        return lambda z, yh: w.at[core, lanes((z % 2) * 1024 + yh * 512 + (z // 2) * 256, 256)]
+
+    def row_land(w):
+        return lambda i: w.at[1 - core, lanes(i * 256, 256)]
+
+    def row_half(v, c):
+        return v.at[lanes(c * 128, 128)]
+
+    gate_sum = GradSum(me, row_slot(wg), row_land(wg), o_gate, 256, row_half, acts, sems(11))
+    up_sum = GradSumY(
+        me, row_slot(wu), row_land(wu), lambda k: hp.at[1 + k // 2, lanes((k % 2) * 256, 256)], o_up, 256, row_half, acts, sems(17)
+    )
+    down_sum = GradSum(
+        me, lambda z, yh: wd.at[core, :, lanes((z % 2) * 1024 + yh * 512 + (z // 2) * 256, 256)],
+        lambda i: wd.at[1 - core, :, lanes(i * 256, 256)], o_down, ff, lambda v, c: v.at[:, lanes(c * 128, 128)], acts, sems(11),
+    )
+    out_sum = GradSum(
+        me, lambda z, yh: wo.at[lanes(core * 256, 256), lanes((z % 2) * 1024 + yh * 512 + (z // 2) * 256, 256)],
+        lambda i: wo.at[lanes((1 - core) * 256, 256), lanes(i * 256, 256)], o_out, 256,
+        lambda v, c: v.at[:, lanes(c * 128, 128)], acts, sems(11),
+    )
+    query_sum = GradSum(
+        me, lambda z, yh: h2.at[pl.ds(0, 256), lanes((z % 2) * 1024 + yh * 512 + (z // 2) * 256, 256)],
+        lambda i: h2.at[pl.ds(256, 256), lanes(i * 256, 256)], o_q, 256,
+        lambda v, c: v.at[:, lanes(c * 128, 128)], acts, sems(11),
+    )
     h2_over.wait()
     for c in hid_over:
         c.wait()
@@ -807,8 +838,12 @@
     back_two_sums[1].turn()
     ring_two[0].turn()
     grads_in(4, 8)
+    shake(7, zs_line + ys_line)
     d_stream(1)
     ring_two[1].start()
+    unshake(7, zs_line + ys_line)
+    up_sum.start()
+    gate_sum.start()
     ring_two[0].finish()
     for h in (0, 1):
         back_two_sums[h].drain()
@@ -885,42 +920,12 @@
     dhf[...] = jnp.zeros(dhf.shape, F32)
     acc[...] = jnp.zeros(acc.shape, F32)
     unshake(0, zs_line + ys_line + four)
-    ff = wg.shape[2]
-    def row_slot(w):
-        return lambda z, yh: w.at[core, lanes((z % 2) * 1024 + yh * 512 + (z // 2) * 256, 256)]
-
-    def row_land(w):
-        return lambda i: w.at[1 - core, lanes(i * 256, 256)]
-
-    def row_half(v, c):
-        return v.at[lanes(c * 128, 128)]
-
-    gate_sum = GradSum(me, row_slot(wg), row_land(wg), o_gate, 256, row_half, acts, sems(11))
-    up_sum = GradSumY(
-        me, row_slot(wu), row_land(wu), lambda k: hp.at[k // 2, lanes((k % 2) * 256, 256)], o_up, 256, row_half, acts, sems(17)
-    )
-    down_sum = GradSum(
-        me, lambda z, yh: wd.at[core, :, lanes((z % 2) * 1024 + yh * 512 + (z // 2) * 256, 256)],
-        lambda i: wd.at[1 - core, :, lanes(i * 256, 256)], o_down, ff, lambda v, c: v.at[:, lanes(c * 128, 128)], acts, sems(11),
-    )
-    out_sum = GradSum(
-        me, lambda z, yh: wo.at[lanes(core * 256, 256), lanes((z % 2) * 1024 + yh * 512 + (z // 2) * 256, 256)],
-        lambda i: wo.at[lanes((1 - core) * 256, 256), lanes(i * 256, 256)], o_out, 256,
-        lambda v, c: v.at[:, lanes(c * 128, 128)], acts, sems(11),
-    )
-    query_sum = GradSum(
-        me, lambda z, yh: h2.at[pl.ds(0, 256), lanes((z % 2) * 1024 + yh * 512 + (z // 2) * 256, 256)],
-        lambda i: h2.at[pl.ds(256, 256), lanes(i * 256, 256)], o_q, 256,
-        lambda v, c: v.at[:, lanes(c * 128, 128)], acts, sems(11),
-    )
-    up_sum.start()
-    gate_sum.start()
     down_sum.start()
     base = sems(5)
     h1_over = send(h1, cfp, acts, base, partner)
-    ot_over = send(ot.at[lanes((1 - core) * 256, 256)], hp.at[2, pl.ds(0, 256), pl.ds(0, 512)], acts, base + 1, partner)
+    ot_over = send(ot.at[lanes((1 - core) * 256, 256)], hp.at[0, pl.ds(0, 256), pl.ds(0, 512)], acts, base + 1, partner)
     da_over = send(mf, h2p, acts, base + 2, partner)
-    dq_over = send(qt.at[lanes((1 - core) * 256, 256)], hp.at[2, pl.ds(256, 256), pl.ds(0, 512)], acts, base + 3, partner)
+    dq_over = send(qt.at[lanes((1 - core) * 256, 256)], hp.at[0, pl.ds(256, 256), pl.ds(0, 512)], acts, base + 3, partner)
     dkv_over = send(dg.at[1, lanes(256 + (1 - core) * 128, 128), pl.ds(0, 512)], o_r.at[pl.ds(0, 128)], acts, base + 4, partner)
     h1_over.start()
     ot_over.start()
@@ -973,39 +978,43 @@
         q = (me.quarter + d) % 4
         for h, k in ((0, q), (1, 7 - q)):
             src = hid.at[k // 4, lanes(((k // 2) % 2) * 256, 256), lanes((k % 2) * 256, 256)]
-            dkv_copies.append(send(src, dkv_slot(dg, (d - 1) * 2 + h), acts, base + h * 4 + d, me.by_quarter(d)))
-    for c in dkv_copies:
-        c.start()
+            copy = send(src, dkv_slot(dg, (d - 1) * 2 + h), acts, base + h * 4 + d, me.by_quarter(d))
+            dkv_copies.append((copy, h == 0 or me.quarter <= q, h == 0 or (me.quarter + 4 - d) % 4 <= me.quarter))
+    for c, goes, _ in dkv_copies:
+        pl.when(goes)(c.start)
     mixed_rows(0)
     mixed_rows(1)
     feed_sums[0].drain()
     feed_sums[1].drain()
     shake(1, [me.by_x(1), me.by_x(3)])
     home_mixed = homeward(mix, o_mixed, sems(4))
-    for c in home_mixed:
-        c.start()
     da_over.wait()
     ot_over.wait()
 
     def out_grad(n, carry):
         cols = lanes(n * 256, 256)
         wo[lanes(core * 256, 256), cols] = (
-            dot_plain(ot[lanes(core * 256, 256), :], mf[:, cols]) + dot_plain(hp[2, 0:256, 0:512], h2p[:, cols])
+            dot_plain(ot[lanes(core * 256, 256), :], mf[:, cols]) + dot_plain(hp[0, 0:256, 0:512], h2p[:, cols])
         ).astype(BF16)
         return carry
 
     lax.fori_loop(0, 8, out_grad, 0)
     shake(3, xs_line + ys_line + zs_line)
+    unshake(3, xs_line + ys_line + zs_line)
+    out_sum.start()
     up_sum.sum_y()
     shake(4, zs_line)
-    for c in dkv_copies:
-        c.wait_recv()
+    for c, _, comes in dkv_copies:
+        pl.when(comes)(c.wait_recv)
     x1[...] = jnp.zeros(x1.shape, F32)
     for h in (0, 1):
         cols = slice(h * CHUNK, (h + 1) * CHUNK)
         total = dhf[:, lanes(chunk_of[h] * CHUNK, CHUNK)]
         for d in range(3):
-            total = total + dkv_slot(dg, d * 2 + h)[...].astype(F32)
+            got_one = dkv_slot(dg, d * 2 + h)[...].astype(F32)
+            if h == 1:
+                got_one = jnp.where((me.quarter + 3 - d) % 4 <= me.quarter, got_one, 0.0)
+            total = total + got_one
         for g in (0, 1):
             a, b = rope_rows(total[g * 64:g * 64 + 32], total[g * 64 + 32:g * 64 + 64], cosine[:, cols], -sine[:, cols])
             v = total[128 + g * 64:192 + g * 64]
@@ -1017,8 +1026,8 @@
             dg[1, 384 + g * 64:448 + g * 64, cols] = v.astype(BF16)
     dkv_over.start()
     du[1, :, 0:512] = x1[...].T.astype(BF16)
-    for c in dkv_copies:
-        c.wait_send()
+    for c, goes, _ in dkv_copies:
+        pl.when(goes)(c.wait_send)
     unstash.wait()
 
     def back_one(h):
@@ -1037,28 +1046,22 @@
 
     row_one = device_order_row(gain1)
     unshake(1, [me.by_x(1), me.by_x(3)])
+    for c in home_mixed:
+        c.start()
     one_sums = ring_sums()
     back_one(0)
     one_sums[0].start()
-    back_one(1)
-    one_sums[1].start()
-    one_sums[0].turn()
     dkv_over.wait()
-    dq_over.wait()
     h1_over.wait()
 
-    def late_grads(n, carry):
+    def kv_grads(n, carry):
         cols = lanes(n * 256, 256)
         mf[256:384, cols] = (
             dot_plain(dg[1, lanes(256 + core * 128, 128), 0:512], h1[:, cols]) + dot_plain(o_r[0:128, :], cfp[:, cols])
         ).astype(BF16)
-        h2[0:256, cols] = (
-            dot_plain(qt[lanes(core * 256, 256), :], h1[:, cols]) + dot_plain(hp[2, 256:512, 0:512], cfp[:, cols])
-        ).astype(BF16)
         return carry
 
-    lax.fori_loop(0, 8, late_grads, 0)
-    unshake(3, xs_line + ys_line + zs_line)
+    lax.fori_loop(0, 8, kv_grads, 0)
     base = sems(25)
     kv_z = [
         send(mf.at[pl.ds(256, 128), lanes(((me.z + d) % 4) * 512, 512)], mf.at[pl.ds(384, 128), pl.ds((d - 1) * 512, 512)],
@@ -1066,8 +1069,8 @@
     ]
     for c in kv_z:
         c.start()
-    out_sum.start()
-    query_sum.start()
+    back_one(1)
+    one_sums[1].start()
     for k in range(2):
         small[k:k + 1, :] = gains[0:1, k * 1024:(k + 1) * 1024]
         small[2 + k:3 + k, :] = gains[1:2, k * 1024:(k + 1) * 1024]
@@ -1087,19 +1090,7 @@
     small_z = small_copies(0, zs_line, sems(3))
     for c in small_z:
         c.start()
-    one_sums[1].turn()
-    unshake(4, zs_line)
-    up_sum.send_z()
-    gate_sum.sum_z()
-    shake(2, ys_line)
-    down_sum.sum_z()
-    shake(5, ys_line)
-
-    def in_rows(h):
-        rows = rows_of(h)
-        dx1[rows, :] += one_sums[h].finish()
-
-    in_rows(0)
+    one_sums[0].turn()
     for c in kv_z:
         c.wait()
     z_at = lanes(me.z * 512, 512)
@@ -1117,17 +1108,20 @@
     small_y = small_copies(1, ys_line, sems(3))
     for c in small_y:
         c.start()
-    in_rows(1)
-    home_in = homeward(dx1, o_in, sems(4))
-    for c in home_in:
-        c.start()
-    unshake(2, ys_line)
-    gate_sum.send_y()
-    unshake(5, ys_line)
-    down_sum.send_y()
-    out_sum.sum_z()
-    query_sum.sum_z()
-    shake(6, ys_line)
+    dq_over.wait()
+
+    def query_grad(n, carry):
+        cols = lanes(n * 256, 256)
+        h2[0:256, cols] = (
+            dot_plain(qt[lanes(core * 256, 256), :], h1[:, cols]) + dot_plain(hp[0, 256:512, 0:512], cfp[:, cols])
+        ).astype(BF16)
+        return carry
+
+    lax.fori_loop(0, 8, query_grad, 0)
+    query_sum.start()
+    one_sums[1].turn()
+    unshake(4, zs_line)
+    up_sum.send_z()
     for c in kv_y:
         c.wait()
     zy_at = lanes(me.z * 512 + me.y * 128, 128)
@@ -1142,13 +1136,15 @@
     small_x = small_copies(2, xs_line, sems(3))
     for c in small_x:
         c.start()
-    unshake(6, ys_line)
-    out_sum.send_y()
-    query_sum.send_y()
-    gate_sum.sum_y()
-    up_sum.sum_z()
+    for c in home_mixed:
+        c.wait()
+
+    def in_rows(h):
+        rows = rows_of(h)
+        mix[rows, :] = (dx1[rows, :] + one_sums[h].finish()).astype(BF16)
+
+    in_rows(0)
     kv_pair.wait()
-    g_rows = lanes((x % 2) * 64, 64)
     mine = mf[pl.ds(pl.multiple_of(256 + (x % 2) * 64, 64), 64), zy_at].astype(F32)
     mine = mine + mf[pl.ds(pl.multiple_of(384 + (x % 2) * 64, 64), 64), 1920:2048].astype(F32)
     head_at = pl.ds(pl.multiple_of((2 * (x % 2) + x // 2) * 64, 64), 64)
@@ -1156,6 +1152,8 @@
     kv_x = [send(mf.at[head_at, zy_at], mf.at[head_at, zy_at], acts, base + 7 + d, me.by_x(d)) for d in (1, 2, 3)]
     for c in kv_x:
         c.start()
+    gate_sum.sum_z()
+    shake(2, ys_line)
     small_add(2, small_x)
     small_c = small_copies(3, [partner], sems(1))
     for c in small_c:
@@ -1166,18 +1164,32 @@
     kv_y2 = [send(block, block, acts, base + 11 + d, me.by_y(d)) for d in (1, 2, 3)]
     for c in kv_y2:
         c.start()
-    down_sum.sum_y()
-    small_add(3, small_c)
+    in_rows(1)
+    home_in = homeward(mix, o_in, sems(4))
+    for c in home_in:
+        c.start()
+    unshake(2, ys_line)
+    gate_sum.send_y()
     for c in kv_y2:
         c.wait()
     block2 = mf.at[pl.ds(0, 256), z_at]
     kv_z2 = [send(block2, block2, acts, base + 15 + d, me.by_z(d)) for d in (1, 2, 3)]
     for c in kv_z2:
         c.start()
-    out_sum.sum_y()
-    query_sum.sum_y()
+    small_add(3, small_c)
     small_out = pltpu.make_async_copy(small, o_small, lsem.at[8])
     small_out.start()
+    down_sum.sum_z()
+    shake(5, ys_line)
+    out_sum.sum_z()
+    query_sum.sum_z()
+    shake(6, ys_line)
+    up_sum.sum_z()
+    unshake(5, ys_line)
+    down_sum.send_y()
+    unshake(6, ys_line)
+    out_sum.send_y()
+    query_sum.send_y()
     for c in kv_z2:
         c.wait()
     kv_last = send(mf.at[pl.ds(0, 256)], mf.at[pl.ds(256, 256)], acts, base + 20, partner)
@@ -1198,27 +1210,31 @@
             flights.append(copy)
 
     lay_out(o_kv.at[core], 0, 0)
+    gate_sum.sum_y()
     kv_last.wait()
     lay_out(o_kv.at[1 - core], 256, 1)
+    down_sum.sum_y()
+    out_sum.sum_y()
+    query_sum.sum_y()
     for c in flights[-4:]:
         c.wait()
     for s in (gate_sum, up_sum, down_sum, out_sum, query_sum):
         s.finish()
-    for c in home_mixed + home_in:
+    for c in home_in:
         c.wait()
     for h in (0, 1):
         one_sums[h].drain()
     small_out.wait()
 
 
-ACTS = 240
+ACTS = 270
 
 
 def layer(tok, cot, wq, wo, wg, wu, wd, w_key, w_value, gain1, gain2, ids):
     ff = wg.shape[1]
     sds = jax.ShapeDtypeStruct
     outs = [
-        sds((1024, 256), BF16), sds((1024, 256), F32), sds((256, 128), BF16), sds((256, 128), BF16),
+        sds((1024, 256), BF16), sds((1024, 256), BF16), sds((256, 128), BF16), sds((256, 128), BF16),
         sds((128, ff), BF16), sds((128, ff), BF16), sds((ff, 128), BF16), sds((2, 2048, 256), F32), sds((8, 1024), F32),
         sds((T, 2048), BF16),
     ]
@@ -1242,7 +1258,7 @@
             inner, inner, inner, pltpu.VMEM((3, T, ff), BF16), pltpu.VMEM((CHUNK, 2048), F32),
             pltpu.VMEM((T, 1), F32), pltpu.VMEM((T, 1), F32), square,
             pltpu.VMEM((2, 2048), F32), pltpu.VMEM((8, 512), F32), pltpu.VMEM((8, 1024), F32), pltpu.VMEM((4, 3, 8, 1024), F32),
-            dma((ACTS,)), dma((ACTS,)), dma((5, 31)), dma((5, 31)), dma((14,)), pltpu.SemaphoreType.REGULAR((8,)),
+            dma((ACTS,)), dma((ACTS,)), dma((5, 31)), dma((5, 31)), dma((14,)), pltpu.SemaphoreType.REGULAR((9,)),
         ],
         compiler_params=pltpu.CompilerParams(collective_id=0, has_side_effects=True, vmem_limit_bytes=64 << 20),
     )(tok, cot, wq, wo, wg, wu, wd, w_key, w_value, gain1, gain2, ids)
@@ -1260,7 +1276,7 @@
     key_total, value_total = gkv[0], gkv[1]
     rms = jnp.sqrt(jnp.sum(small[4:7, :512], 1) / (16384 * 2048))
     return (
-        mixed, input_grad, gq.T.astype(F32), key_total, value_total, go.astype(F32), gg.astype(F32), gu.astype(F32),
+        mixed, input_grad.astype(F32), gq.T.astype(F32), key_total, value_total, go.astype(F32), gg.astype(F32), gu.astype(F32),
         gd.astype(F32), from_device_order(small[0:2].reshape(2048)), from_device_order(small[2:4].reshape(2048)), rms,
     )
 

time: 366 us -> 327 us (0.89)
  Pallas kernels: 345 us -> 306 us
    pallas_call x1, Pallas kernels: 345 us -> 306 us  [layer(): pl.pallas_call(layer_kernel, out_shape=outs, in_specs=[ANY] * 7 + [vm] *...]
    unnamed x23 -> x22, local copies, waits for them, and re-layouts: 8.97 us -> 8 us
where the time goes in v3:
time: 327 us
  Pallas kernels  306 us (94%)
  local copies, waits for them, and re-layouts  16 us (5%)
  other arithmetic  3.93 us (1%)
    pallas_call x1, Pallas kernels, layer(): pl.pallas_call(layer_kernel, out_shape=outs, in_specs=[ANY] * 7 + [vm] *...  306 us
    unnamed x22, local copies, waits for them, and re-layouts  8 us

profile of v3, /device:TPU:1, one launch (start us, length us, event | category | flops | bytes accessed | tf_op | source)
XLA Modules:
  0.0 326.6 jit_solution(11328168945396764138)
XLA Ops:
  0.6 1.7 copy.29.wg_s
  2.4 1.7 copy.30.wu_s
  4.1 1.3 reshape.39.gain1
  5.4 1.3 reshape.40.gain2
  6.7 305.9 %shard_map.211 = (bf16[1024,256]{1,0:T(8,128)(2,1)}, bf16[1024,256]{1,0:T(8,128)(2,1)}, bf16[256,128]{1,0:T(8,128)(2,1)}, bf16[256,128]{1,0:T(8,128)(2,1)}, bf16...) custom-call(bf16[1024,256]{1,0:T(8,128)(2,1)} %tok.1, ...), custom_call_target="tpu_custom_call" | custom-call | tf_op jit(solution)/shard_map/pallas_call | solution.py:1248
  312.7 0.8 fusion
  313.5 0.6 copy.36
  314.2 0.6 copy.37
  314.8 0.0 copy-start
  314.8 0.0 copy-start.4
  314.8 4.6 %slice_bitcast_fusion = (f32[2048,256]{1,0:T(8,128)}, f32[2048,256]{1,0:T(8,128)}) fusion(f32[2,2048,256]{2,1,0:T(8,128)} %get-tuple-element.24), kind=kLoop, calls=%fused_computation | loop fusion | bytes 8388608 | tf_op jit(solution)/shard_map/squeeze | solution.py:1276
  319.3 0.0 copy-start.3
  319.3 0.0 copy-start.2
  319.3 0.0 copy-start.6
  319.3 0.0 copy-start.5
  319.4 0.0 copy-start.1
  319.4 0.9 slice_reduce_fusion
  320.3 0.5 multiply_sqrt_fusion
  320.8 0.0 copy-done
  320.8 1.0 convert_element_type.21
  321.9 0.0 copy-done.4
  321.9 0.8 convert_element_type.27
  322.6 0.0 copy-done.3
  322.6 0.9 copy.34
  323.5 0.0 copy-done.2
  323.5 0.9 copy.35
  324.4 0.0 copy-done.6
  324.4 0.8 copy.33
  325.1 0.0 copy-done.5
  325.1 0.7 convert_element_type.24
  325.8 0.0 copy-done.1
  325.8 0.8 copy.43
  (5 shorter events, 0.1 us)
Async XLA Ops:
  314.8 6.0 %copy-start = (bf16[1024,256]{1,0:T(8,128)(2,1)S(1)}, bf16[1024,256]{1,0:T(8,128)(2,1)}, u32[]{:S(2)}) copy-start(bf16[1024,256]{1,0:T(8,128)(2,1)} %get-tuple-element.22) | copy-start | bytes 1572868
  314.8 7.1 %copy-start.4 = (bf16[704,128]{1,0:T(8,128)(2,1)S(1)}, bf16[704,128]{1,0:T(8,128)(2,1)}, u32[]{:S(2)}) copy-start(bf16[704,128]{1,0:T(8,128)(2,1)} %get-tuple-element.28) | copy-start | bytes 540676
  319.3 3.3 %copy-start.3 = (bf16[128,704]{1,0:T(8,128)(2,1)S(1)}, bf16[128,704]{1,0:T(8,128)(2,1)}, u32[]{:S(2)}) copy-start(bf16[128,704]{1,0:T(8,128)(2,1)} %get-tuple-element.26) | copy-start | bytes 540676
  319.3 4.2 %copy-start.2 = (bf16[128,704]{1,0:T(8,128)(2,1)S(1)}, bf16[128,704]{1,0:T(8,128)(2,1)}, u32[]{:S(2)}) copy-start(bf16[128,704]{1,0:T(8,128)(2,1)} %get-tuple-element.27) | copy-start | bytes 540676
  319.3 5.0 %copy-start.6 = (bf16[256,128]{1,0:T(8,128)(2,1)S(1)}, bf16[256,128]{1,0:T(8,128)(2,1)}, u32[]{:S(2)}) copy-start(bf16[256,128]{1,0:T(8,128)(2,1)} %get-tuple-element.23) | copy-start | bytes 196612
  319.3 5.8 %copy-start.5 = (bf16[256,128]{1,0:T(8,128)(2,1)S(1)}, bf16[256,128]{1,0:T(8,128)(2,1)}, u32[]{:S(2)}) copy-start(bf16[256,128]{1,0:T(8,128)(2,1)} %get-tuple-element.25) | copy-start | bytes 196612
  319.4 6.5 %copy-start.1 = (bf16[1024,256]{1,0:T(8,128)(2,1)S(1)}, bf16[1024,256]{1,0:T(8,128)(2,1)}, u32[]{:S(2)}) copy-start(bf16[1024,256]{1,0:T(8,128)(2,1)} %get-tuple-element.70) | copy-start | bytes 1572868

commit v4 on v3

--- a/solution.py
+++ b/solution.py
@@ -1001,7 +1001,6 @@
     lax.fori_loop(0, 8, out_grad, 0)
     shake(3, xs_line + ys_line + zs_line)
     unshake(3, xs_line + ys_line + zs_line)
-    out_sum.start()
     up_sum.sum_y()
     shake(4, zs_line)
     for c, _, comes in dkv_copies:
@@ -1119,6 +1118,7 @@
 
     lax.fori_loop(0, 8, query_grad, 0)
     query_sum.start()
+    out_sum.start()
     one_sums[1].turn()
     unshake(4, zs_line)
     up_sum.send_z()

time: 327 us -> 324 us (level)
  no operation moved by 1% of the time
where the time goes in v4:
time: 324 us
  Pallas kernels  303 us (94%)
  local copies, waits for them, and re-layouts  16 us (5%)
  other arithmetic  3.93 us (1%)
    pallas_call x1, Pallas kernels, layer(): pl.pallas_call(layer_kernel, out_shape=outs, in_specs=[ANY] * 7 + [vm] *...  303 us
    unnamed x22, local copies, waits for them, and re-layouts  8 us

profile of v4, /device:TPU:1, one launch (start us, length us, event | category | flops | bytes accessed | tf_op | source)
XLA Modules:
  0.0 324.1 jit_solution(9628506979002419417)
XLA Ops:
  0.6 1.7 copy.29.wg_s
  2.4 1.7 copy.30.wu_s
  4.1 1.3 reshape.39.gain1
  5.4 1.3 reshape.40.gain2
  6.7 303.4 %shard_map.211 = (bf16[1024,256]{1,0:T(8,128)(2,1)}, bf16[1024,256]{1,0:T(8,128)(2,1)}, bf16[256,128]{1,0:T(8,128)(2,1)}, bf16[256,128]{1,0:T(8,128)(2,1)}, bf16...) custom-call(bf16[1024,256]{1,0:T(8,128)(2,1)} %tok.1, ...), custom_call_target="tpu_custom_call" | custom-call | tf_op jit(solution)/shard_map/pallas_call | solution.py:1248
  310.1 0.8 fusion
  311.0 0.6 copy.36
  311.6 0.6 copy.37
  312.2 0.0 copy-start
  312.2 0.0 copy-start.4
  312.2 4.6 %slice_bitcast_fusion = (f32[2048,256]{1,0:T(8,128)}, f32[2048,256]{1,0:T(8,128)}) fusion(f32[2,2048,256]{2,1,0:T(8,128)} %get-tuple-element.24), kind=kLoop, calls=%fused_computation | loop fusion | bytes 8388608 | tf_op jit(solution)/shard_map/squeeze | solution.py:1276
  316.8 0.0 copy-start.3
  316.8 0.0 copy-start.2
  316.8 0.0 copy-start.6
  316.8 0.0 copy-start.5
  316.8 0.0 copy-start.1
  316.8 0.9 slice_reduce_fusion
  317.7 0.5 multiply_sqrt_fusion
  318.3 0.0 copy-done
  318.3 1.0 convert_element_type.21
  319.3 0.0 copy-done.4
  319.3 0.8 convert_element_type.27
  320.1 0.0 copy-done.3
  320.1 0.9 copy.34
  320.9 0.0 copy-done.2
  320.9 0.9 copy.35
  321.8 0.0 copy-done.6
  321.8 0.8 copy.33
  322.6 0.0 copy-done.5
  322.6 0.7 convert_element_type.24
  323.3 0.0 copy-done.1
  323.3 0.8 copy.43
  (5 shorter events, 0.1 us)
Async XLA Ops:
  312.2 6.0 %copy-start = (bf16[1024,256]{1,0:T(8,128)(2,1)S(1)}, bf16[1024,256]{1,0:T(8,128)(2,1)}, u32[]{:S(2)}) copy-start(bf16[1024,256]{1,0:T(8,128)(2,1)} %get-tuple-element.22) | copy-start | bytes 1572868
  312.2 7.1 %copy-start.4 = (bf16[704,128]{1,0:T(8,128)(2,1)S(1)}, bf16[704,128]{1,0:T(8,128)(2,1)}, u32[]{:S(2)}) copy-start(bf16[704,128]{1,0:T(8,128)(2,1)} %get-tuple-element.28) | copy-start | bytes 540676
  316.8 3.3 %copy-start.3 = (bf16[128,704]{1,0:T(8,128)(2,1)S(1)}, bf16[128,704]{1,0:T(8,128)(2,1)}, u32[]{:S(2)}) copy-start(bf16[128,704]{1,0:T(8,128)(2,1)} %get-tuple-element.26) | copy-start | bytes 540676
  316.8 4.2 %copy-start.2 = (bf16[128,704]{1,0:T(8,128)(2,1)S(1)}, bf16[128,704]{1,0:T(8,128)(2,1)}, u32[]{:S(2)}) copy-start(bf16[128,704]{1,0:T(8,128)(2,1)} %get-tuple-element.27) | copy-start | bytes 540676
  316.8 5.0 %copy-start.6 = (bf16[256,128]{1,0:T(8,128)(2,1)S(1)}, bf16[256,128]{1,0:T(8,128)(2,1)}, u32[]{:S(2)}) copy-start(bf16[256,128]{1,0:T(8,128)(2,1)} %get-tuple-element.23) | copy-start | bytes 196612
  316.8 5.8 %copy-start.5 = (bf16[256,128]{1,0:T(8,128)(2,1)S(1)}, bf16[256,128]{1,0:T(8,128)(2,1)}, u32[]{:S(2)}) copy-start(bf16[256,128]{1,0:T(8,128)(2,1)} %get-tuple-element.25) | copy-start | bytes 196612
  316.8 6.5 %copy-start.1 = (bf16[1024,256]{1,0:T(8,128)(2,1)S(1)}, bf16[1024,256]{1,0:T(8,128)(2,1)}, u32[]{:S(2)}) copy-start(bf16[1024,256]{1,0:T(8,128)(2,1)} %get-tuple-element.70) | copy-start | bytes 1572868
